TPU v7x, 256 devices: a whole 4x4x8 slice. The times are simulated.
256 devices in a mesh: leaf: 8 (over x, core), ctx: 8 (over z), head: 4 (over y).
Axes of the slice: x: 4, y: 4, z: 8, core: 2. Of those that a mesh axis runs over, the one named last changes fastest.
Arguments:
- queries: bfloat16 [16384, 8192], P(('leaf', 'ctx'), 'head')
- inputs: bfloat16 [16384, 5120], P(('leaf', 'ctx'), 'head'), may hold values from -6 to 6
- key_weight: bfloat16 [5120, 1024], P(None, 'head'), may hold values from -0.078125 to 0.078125
- value_weight: bfloat16 [5120, 1024], P(None, 'head'), may hold values from -0.078125 to 0.078125
- parents: int32 [128], replicated, may hold values from -1 to 126, as said below
- tile_dest: int32 [512], replicated, may hold values from 0 to 511, as said below
Outputs:
- placed: bfloat16 [16384, 8192], P(('leaf', 'ctx'), 'head')
Inputs may be any that keep to these rules, and one draw needn't show every extreme that they name: parents[0] = -1, every later segment's parent is an earlier segment, and the last segment's parent is the segment just before it. `tile_dest`: a permutation; the tiles of block b (tiles b * 8 to b * 8 + 7) go to blocks of the same group of 8 consecutive blocks; from one block to one block go at most 2 tiles, and exactly 2 for some pairs in every group.
All inputs are finite; a program needn't handle non-finite values.
Results may differ from a plain program's by a relative error of at most 0.006.
The roundings to bfloat16 on the way count: a program that leaves them out, or rounds other values in their place, can miss the bound.
Values may be sent and summed in bfloat16 or wider, within the bound.
No kernel may reach another device: no remote copies, remote signals or barrier semaphores. Data moves between devices by JAX's collectives and lax.ppermute only.
A program may use at most 128 MiB of HBM per device.

v0:
```python
import functools
import math

import jax
import jax.numpy as jnp
from jax import lax
from jax.experimental import pallas as pl
from jax.experimental.pallas import tpu as pltpu
from jax.sharding import PartitionSpec as P

HEAD = 128
GROUP = 8
SEG = 128
TILE = 32
TPD = 8
CAP = 2
NX, NZ, NY = 4, 8, 4
ROWS = TILE * GROUP
SCALE = math.log2(math.e) / math.sqrt(HEAD)
FILL = -1.2e31
MIB = 1 << 20
UNIT = 4
LIST = 32 + 16
PASSES = 5

XP = [(2 * x + c, 2 * ((x + 1) % NX) + c) for x in range(NX) for c in range(2)]
XM = [(2 * x + c, 2 * ((x - 1) % NX) + c) for x in range(NX) for c in range(2)]
CS = [(i, i ^ 1) for i in range(2 * NX)]


def turn(n, by):
    return [(i, (i + by) % n) for i in range(n)]


ZP, ZM = turn(NZ, 1), turn(NZ, -1)
YP, YM = turn(NY, 1), turn(NY, -1)

smem = functools.partial(pl.BlockSpec, memory_space=pltpu.SMEM)
vmem = functools.partial(pl.BlockSpec, memory_space=pltpu.VMEM)


def pack_kernel(where, dest, q, *outs):
    sends, table, info = outs[:NZ], outs[NZ], outs[NZ + 1]
    leaf, ctx = where[0], where[1]
    device = leaf * NZ + ctx
    shifts = [((dest[device * TPD + j] >> 3) - ctx) & (NZ - 1) for j in range(TPD)]
    ranks = []
    for j in range(TPD):
        rank = jnp.int32(0)
        for i in range(j):
            rank = rank + (shifts[i] == shifts[j]).astype(jnp.int32)
        ranks.append(rank)
    for s in range(NZ):
        for r in range(CAP):
            pick = jnp.int32(0)
            for j in range(TPD):
                pick = jnp.where((shifts[j] == s) & (ranks[j] == r), j, pick)
            sends[s][r] = q[pl.ds(pl.multiple_of(pick * TILE, TILE), TILE), :]
    for s in range(NZ):
        base = (leaf * NZ + ((ctx - s) & (NZ - 1))) * TPD
        table[s * CAP] = jnp.int32(-1)
        table[s * CAP + 1] = jnp.int32(-1)

        def one(j, rank, s=s, base=base):
            to = dest[base + j]
            mine = (to >> 3) == device

            @pl.when(mine)
            def _():
                table[s * CAP + rank] = to & (TPD - 1)
                info[to & (TPD - 1)] = base + j

            return rank + mine.astype(jnp.int32)

        lax.fori_loop(0, TPD, one, jnp.int32(0))


def pack(where, dest, q):
    width = q.shape[1]
    outs = pl.pallas_call(
        pack_kernel,
        in_specs=[smem(), smem(), vmem()],
        out_specs=[vmem()] * NZ + [smem(), smem()],
        out_shape=[jax.ShapeDtypeStruct((CAP, TILE, width), q.dtype)] * NZ
        + [jax.ShapeDtypeStruct((NZ * CAP,), jnp.int32), jax.ShapeDtypeStruct((TPD,), jnp.int32)],
        compiler_params=pltpu.CompilerParams(vmem_limit_bytes=32 * MIB),
        cost_estimate=pl.CostEstimate(flops=0, bytes_accessed=3 * MIB, transcendentals=0),
        name="pack",
    )(where, dest, q)
    return outs[:NZ], outs[NZ], outs[NZ + 1]


def walk_kernel(parents, info, which, place, lists, counts):
    def tile(d, carry):
        for p in range(PASSES):
            counts[p * TPD + d] = jnp.int32(0)

        def body(at):
            row = which[at] * TPD + d
            used = counts[row]
            lists[row * LIST + used] = place[at]
            counts[row] = used + 1
            return parents[at]

        seg = info[d] >> 2
        lax.while_loop(lambda at: at >= 0, body, seg)
        counts[PASSES * TPD + d] = which[seg]
        for p in range(PASSES):
            row = p * TPD + d
            used = row * LIST + counts[row]
            for n in range(2 * UNIT):
                lists[used + n] = jnp.int32(0)
        return carry

    lax.fori_loop(0, TPD, tile, 0)


def walk(parents, info, which, place):
    return pl.pallas_call(
        walk_kernel,
        in_specs=[smem()] * 4,
        out_specs=[smem()] * 2,
        out_shape=[
            jax.ShapeDtypeStruct((PASSES * TPD * LIST,), jnp.int32),
            jax.ShapeDtypeStruct(((PASSES + 1) * TPD,), jnp.int32),
        ],
        cost_estimate=pl.CostEstimate(flops=0, bytes_accessed=16 * MIB, transcendentals=0),
        name="walk",
    )(parents, info, which, place)


def unpack_kernel(table, *refs):
    came, out = refs[:NZ], refs[NZ]
    for s in range(NZ):

        def one(r, carry, s=s):
            d = table[s * CAP + r]

            @pl.when(d >= 0)
            def _():
                for g in range(2):
                    heads = [
                        came[s][r, :, pl.ds((g * GROUP + h) * HEAD, HEAD)] for h in range(GROUP)
                    ]
                    out[d, g] = jnp.concatenate(heads, axis=0).T

            return carry

        lax.fori_loop(0, CAP, one, 0)


def unpack(table, came):
    return pl.pallas_call(
        unpack_kernel,
        in_specs=[smem()] + [vmem()] * NZ,
        out_specs=vmem(),
        out_shape=jax.ShapeDtypeStruct((TPD, 2, HEAD, ROWS), jnp.bfloat16),
        compiler_params=pltpu.CompilerParams(vmem_limit_bytes=32 * MIB),
        cost_estimate=pl.CostEstimate(flops=0, bytes_accessed=6 * MIB, transcendentals=0),
        name="unpack",
    )(table, *came)


def project_kernel(where, own, before, after, far0, far1, wk, wv, out):
    y = where[2]
    depth = own.shape[1]
    half = far0.shape[0]

    def rows(by):
        at = (y + by) & (NY - 1)
        return pl.ds(pl.multiple_of(at * depth, depth), depth)

    def times(w):
        total = jnp.dot(own[...], w[rows(0), :], preferred_element_type=jnp.float32)
        total += jnp.dot(before[...], w[rows(NY - 1), :], preferred_element_type=jnp.float32)
        total += jnp.dot(after[...], w[rows(1), :], preferred_element_type=jnp.float32)
        far = jnp.concatenate([far0[...], far1[...]], axis=0)
        return total + jnp.dot(far, w[rows(2), :], preferred_element_type=jnp.float32)

    k = times(wk)
    v = times(wv)
    for n in range(2):
        at = n * 2 * SEG
        out[at : at + SEG, :] = k[n * SEG : (n + 1) * SEG].astype(out.dtype)
        for g in range(2):
            part = v[n * SEG : (n + 1) * SEG, g * HEAD : (g + 1) * HEAD]
            out[at + SEG : at + 2 * SEG, g * HEAD : (g + 1) * HEAD] = part.T.astype(out.dtype)


def project(where, own, before, after, far0, far1, wk, wv):
    return pl.pallas_call(
        project_kernel,
        in_specs=[smem()] + [vmem()] * 7,
        out_specs=vmem(),
        out_shape=jax.ShapeDtypeStruct((4 * SEG, 2 * HEAD), jnp.bfloat16),
        compiler_params=pltpu.CompilerParams(vmem_limit_bytes=40 * MIB),
        cost_estimate=pl.CostEstimate(flops=2 * 256 * 5120 * 512, bytes_accessed=8 * MIB, transcendentals=0),
        name="project",
    )(where, own, before, after, far0, far1, wk, wv)


def attend_kernel(which, n_pieces, lists, counts, info, qt, *refs):
    pieces, refs = refs[:n_pieces], refs[n_pieces:]
    first, finish = which == 0, which == PASSES - 1
    if not first:
        old_top, old_total, old_sum, refs = *refs[:3], refs[3:]
    if finish:
        out, kv, score, peak, weight, sems, top, total, acc = refs
    else:
        top, total, acc, kv, score, peak, weight, sems = refs
    copies, at = [], 0
    for n, piece in enumerate(pieces):
        size = piece.shape[0]
        copies.append(pltpu.make_async_copy(piece, kv.at[pl.ds(at, size)], sems.at[n]))
        at += size
    for copy in copies:
        copy.start()
    for copy in copies:
        copy.wait()

    def keys(w, g):
        return kv[w, 0:SEG, g * HEAD : (g + 1) * HEAD]

    def tile(d, carry):
        base = (which * TPD + d) * LIST
        count = counts[which * TPD + d]
        ids = [d * 2 + g for g in range(2)]

        def spots(i):
            return [lists[base + i * UNIT + u] for u in range(UNIT)]

        def scores(places, limit=None):
            for g in range(2):
                k = jnp.concatenate([keys(w, g) for w in places], axis=0)
                s = jnp.dot(k, qt[d, g], preferred_element_type=jnp.float32)
                if limit is not None:
                    key = lax.broadcasted_iota(jnp.int32, (UNIT * SEG, ROWS), 0)
                    s = jnp.where((key <= limit) | (key >= SEG), s, FILL)
                score[g] = s
                for u in range(UNIT):
                    part = s[u * SEG : (u + 1) * SEG].reshape(SEG // 8, 8, ROWS)
                    peak[g, u] = jnp.max(part, axis=0)

        for g in range(2):
            i = ids[g]
            if not first:
                top[i], total[i], acc[i] = old_top[i], old_total[i], old_sum[i]
            else:
                top[i] = jnp.full((1, ROWS), FILL, jnp.float32)
                total[i] = jnp.zeros((1, ROWS), jnp.float32)
                acc[i] = jnp.zeros((HEAD, ROWS), jnp.float32)
            weight[g] = jnp.zeros_like(weight[g])
        own, quarter = counts[PASSES * TPD + d] == which, info[d] & 3
        token = lax.broadcasted_iota(jnp.int32, (UNIT * SEG, ROWS), 1) & (TILE - 1)
        scores(spots(0), token + jnp.where(own, quarter * TILE, SEG))
        def add(places, drops):
            for g in range(2):
                v = jnp.concatenate(
                    [kv[w, SEG : 2 * SEG, g * HEAD : (g + 1) * HEAD] for w in places], axis=1
                )
                acc[ids[g]] = acc[ids[g]] * drops[g] + jnp.dot(
                    v, weight[g], preferred_element_type=jnp.float32
                )

        def body(i, drops):
            later = spots(i + 1)
            pens = [jnp.where(i * UNIT + u < count, 0.0, 3e31) for u in range(UNIT)]
            result = []
            add(spots(jnp.maximum(i - 1, 0)), drops)
            for g in range(2):
                old = top[ids[g]]
                peaks = [
                    peak[g, u] - pens[u] for u in range(UNIT)
                ]
                peaks = jnp.max(functools.reduce(jnp.maximum, peaks), axis=0, keepdims=True)
                new = jnp.maximum(old, peaks)
                drop = jnp.exp2((old - new) * SCALE)
                part = jnp.zeros((8, ROWS), jnp.float32)
                for u in range(UNIT):
                    e = jnp.exp2((score[g, u * SEG : (u + 1) * SEG] - (new + pens[u])) * SCALE)
                    part += jnp.sum(e.reshape(SEG // 8, 8, ROWS), axis=0)
                    weight[g, u * SEG : (u + 1) * SEG] = e.astype(jnp.bfloat16)
                total[ids[g]] = total[ids[g]] * drop + jnp.sum(part, axis=0, keepdims=True)
                top[ids[g]] = new
                result.append(drop)
            scores(later)
            return tuple(result)

        rounds = (count + UNIT - 1) // UNIT
        ones = jnp.ones((1, ROWS), jnp.float32)
        drops = lax.fori_loop(0, rounds, body, (ones, ones))
        add(spots(jnp.maximum(rounds - 1, 0)), drops)

        if finish:
            for g in range(2):
                i = ids[g]
                o = (acc[i] / total[i]).T.astype(out.dtype)
                for h in range(GROUP):
                    out[
                        pl.ds(pl.multiple_of(d * TILE, TILE), TILE),
                        (g * GROUP + h) * HEAD : (g * GROUP + h + 1) * HEAD,
                    ] = o[h * TILE : (h + 1) * TILE]
        return carry

    lax.fori_loop(0, TPD, tile, 0)


def attend(which, lists, counts, info, qt, pieces, state):
    first, finish = which == 0, which == PASSES - 1
    shapes = [
        jax.ShapeDtypeStruct((2 * TPD, 1, ROWS), jnp.float32),
        jax.ShapeDtypeStruct((2 * TPD, 1, ROWS), jnp.float32),
        jax.ShapeDtypeStruct((2 * TPD, HEAD, ROWS), jnp.float32),
    ]
    result = jax.ShapeDtypeStruct((TPD * TILE, 2 * GROUP * HEAD), jnp.bfloat16)
    blocks = sum(piece.shape[0] for piece in pieces)
    scratch = [
        pltpu.VMEM((blocks, 2 * SEG, 2 * HEAD), jnp.bfloat16),
        pltpu.VMEM((2, UNIT * SEG, ROWS), jnp.float32),
        pltpu.VMEM((2, UNIT, 8, ROWS), jnp.float32),
        pltpu.VMEM((2, UNIT * SEG, ROWS), jnp.bfloat16),
        pltpu.SemaphoreType.DMA((len(pieces),)),
    ]
    if finish:
        scratch += [pltpu.VMEM(a.shape, a.dtype) for a in shapes]
    return pl.pallas_call(
        functools.partial(attend_kernel, which, len(pieces)),
        in_specs=[smem()] * 3
        + [vmem()]
        + [pl.BlockSpec(memory_space=pl.ANY)] * len(pieces)
        + [vmem()] * (0 if first else 3),
        out_specs=vmem() if finish else [vmem()] * 3,
        out_shape=result if finish else shapes,
        scratch_shapes=scratch,
        compiler_params=pltpu.CompilerParams(vmem_limit_bytes=28 * MIB),
        cost_estimate=pl.CostEstimate(
            flops=256 * 16 * 128 * 128 * 32, bytes_accessed=6 * MIB, transcendentals=0
        ),
        name="attend",
    )(lists, counts, info, qt, *pieces, *(() if first else state))


def cat(*parts):
    return jnp.concatenate(parts, axis=0)


def ring_four(block, axis, up, down, ready=()):
    half = block.shape[0] // 2
    low = lax.ppermute(block, axis, up)
    high = lax.ppermute(block, axis, down)
    low, high, _ = lax.optimization_barrier((low, high, ready))
    far0 = lax.ppermute(low[:half], axis, up)
    far1 = lax.ppermute(high[half:], axis, down)
    return [block, low, high, far0, far1]


def swapped(pieces):
    pieces = pieces + [lax.ppermute(a, "leaf", CS) for a in pieces]
    return [a.reshape(-1, 2 * SEG, 2 * HEAD) for a in pieces]


def on_device(queries, inputs, key_weight, value_weight, parents, tile_dest):
    leaf, ctx, y = lax.axis_index("leaf"), lax.axis_index("ctx"), lax.axis_index("head")
    where = jnp.stack([leaf, ctx, y]).astype(jnp.int32)
    sends, table, info = pack(where, tile_dest, queries)
    came = [sends[0]] + [lax.ppermute(sends[s], "ctx", turn(NZ, s)) for s in range(1, NZ)]
    rows = ring_four(inputs, "head", YP, YM, sends)

    seg = jnp.arange(parents.shape[0], dtype=jnp.int32)
    block = seg >> 1
    from_leaf, from_z = block >> 3, block & (NZ - 1)
    z = (from_z - ctx) & (NZ - 1)
    x = ((from_leaf >> 1) - (leaf >> 1)) & (NX - 1)
    x = jnp.where(x == 0, 0, jnp.where(x == 1, 2, jnp.where(x == 2, 3, 1)))
    which = jnp.where(z <= 4, z, NZ - z)
    side = jnp.where((which == 0) | (which == 4), 0, jnp.where(z < 4, 1, 0))
    span = jnp.where((which == 0) | (which == 4), 8, 16)
    place = x * 2 + (seg & 1) + side * 8 + span * ((from_leaf ^ leaf) & 1)
    lists, counts = walk(parents, info, which, place)
    rows, lists, counts = lax.optimization_barrier((rows, lists, counts))

    plane = cat(*ring_four(project(where, *rows, key_weight, value_weight), "leaf", XP, XM))
    qt = unpack(table, came)
    plane, qt = lax.optimization_barrier((plane, qt))

    low = high = plane
    pieces, state = [plane], None
    for p in range(PASSES - 1):
        half = plane.shape[0] // 2
        if p < PASSES - 2:
            low, high = lax.ppermute(low, "ctx", ZP), lax.ppermute(high, "ctx", ZM)
        else:
            low, high = lax.ppermute(low[:half], "ctx", ZP), lax.ppermute(high[half:], "ctx", ZM)
        state = attend(p, lists, counts, info, qt, swapped(pieces), state)
        low, high, state = lax.optimization_barrier((low, high, state))
        pieces = [low, high]
    return attend(PASSES - 1, lists, counts, info, qt, swapped(pieces), state)


def solution(mesh):
    in_specs = (
        P(("leaf", "ctx"), "head"),
        P(("leaf", "ctx"), "head"),
        P(None, "head"),
        P(None, "head"),
        P(),
        P(),
    )
    out_specs = P(("leaf", "ctx"), "head")
    return jax.shard_map(
        on_device, mesh=mesh, in_specs=in_specs, out_specs=out_specs, check_vma=False
    )
```

profile of v0, /device:TPU:37, one launch (start us, length us, event | category | flops | bytes accessed | tf_op | source)
XLA Modules:
  0.0 205.5 jit_solution(9193025840176996979)
XLA Ops:
  0.0 1.3 collective-permute-start
  1.3 1.4 collective-permute-start.1
  2.7 0.1 pad_add_fusion.where
  2.8 1.2 copy-done.2
  4.0 0.7 copy-done.4
  4.7 2.3 %pack.1 = (bf16[2,32,2048]{2,1,0:T(8,128)(2,1)S(1)}, bf16[2,32,2048]{2,1,0:T(8,128)(2,1)S(1)}, bf16[2,32,2048]{2,1,0:T(8,128)(2,1)S(1)}, bf16[2,32,2048]{2,1,0:T...) custom-call(s32[3]{0:T(128)S(1)} %pad_add_fusion.where, ...), custom_call_target="tpu_custom_call" | custom-call | bytes 3145728 | tf_op jit(solution)/shard_map/pack/pallas_call | solution.py:80
  7.1 10.0 %collective-permute-done.before = bf16[256,1280]{1,0:T(8,128)(2,1)S(1)} collective-permute-done((bf16[256,1280]{1,0:T(8,128)(2,1)}, bf16[256,1280]{1,0:T(8,128)(2,1)S(1)}, u32[]{:S(2)}, u32[]{:S(2)}) %collective-permute-start) | collective-permute-done | bytes 655392 | tf_op jit(solution)/shard_map/ppermute | solution.py:349
  17.2 1.0 collective-permute-start.2
  18.2 0.7 slice.19
  18.9 1.7 collective-permute-start.3
  20.7 5.6 %collective-permute-start.10 = (bf16[2,32,2048]{2,1,0:T(8,128)(2,1)}, bf16[2,32,2048]{2,1,0:T(8,128)(2,1)S(1)}, u32[]{:S(2)}, u32[]{:S(2)}) collective-permute-start(bf16[2,32,2048]{2,1,0:T(8,128)(2,1)} %get-tuple-element.65), channel_id=1, source_target_pairs={{0,12},{4,16},{8,20},{12,24},{16,28},{20,0},{24,4},{28,8},{1,13},{... | collective-permute-start | bytes 786440 | tf_op jit(solution)/shard_map/ppermute | solution.py:366
  26.2 0.5 collective-permute-start.11
  26.7 4.5 %collective-permute-start.12 = (bf16[2,32,2048]{2,1,0:T(8,128)(2,1)}, bf16[2,32,2048]{2,1,0:T(8,128)(2,1)}, u32[]{:S(2)}, u32[]{:S(2)}) collective-permute-start(bf16[2,32,2048]{2,1,0:T(8,128)(2,1)} %get-tuple-element.67), channel_id=1, source_target_pairs={{0,20},{4,24},{8,28},{12,0},{16,4},{20,8},{24,12},{28,16},{1,21},{... | collective-permute-start | bytes 786440 | tf_op jit(solution)/shard_map/ppermute | solution.py:366
  31.2 0.2 collective-permute-start.13
  31.4 0.6 compare_select_fusion
  32.0 5.7 %walk.1 = (s32[1920]{0:T(1024)}, s32[48]{0:T(128)}) custom-call(s32[128]{0:T(128)} %parents.1, s32[8]{0:T(128)} %copy-done.5, s32[128]{0:T(128)} %get-tuple-element.119.which, s32[128]{0:T(128)} %get-tuple-element.120.place), custom_call_target="tpu_custom_call" | custom-call | bytes 16777216 | tf_op jit(solution)/shard_map/walk/pallas_call | solution.py:119
  37.7 0.7 collective-permute-start.14
  38.3 6.5 %collective-permute-done.10.refs_3_ = bf16[2,32,2048]{2,1,0:T(8,128)(2,1)S(1)} collective-permute-done((bf16[2,32,2048]{2,1,0:T(8,128)(2,1)}, bf16[2,32,2048]{2,1,0:T(8,128)(2,1)S(1)}, u32[]{:S(2)}, u32[]{:S(2)}) %collective-permute-start.10) | collective-permute-done | bytes 262176 | tf_op jit(solution)/shard_map/ppermute | solution.py:366
  44.8 4.3 %collective-permute-start.9 = (bf16[2,32,2048]{2,1,0:T(8,128)(2,1)}, bf16[2,32,2048]{2,1,0:T(8,128)(2,1)S(1)}, u32[]{:S(2)}, u32[]{:S(2)}) collective-permute-start(bf16[2,32,2048]{2,1,0:T(8,128)(2,1)} %copy-done.7), channel_id=1, source_target_pairs={{0,8},{4,12},{8,16},{12,20},{16,24},{20,28},{24,0},{28,4},{1,9},{5... | collective-permute-start | bytes 786440 | tf_op jit(solution)/shard_map/ppermute | solution.py:366
  49.1 1.7 copy-done
  50.8 1.7 copy-done.1
  52.6 2.1 %project.1 = bf16[512,256]{1,0:T(8,128)(2,1)S(1)} custom-call(s32[3]{0:T(128)S(1)} %pad_add_fusion.where, bf16[256,1280]{1,0:T(8,128)(2,1)S(1)} %copy-done.3, bf16[256,1280]{1,0:T(8,128)(2,1)S(1)} %collective-permute-done.before, bf16[256,1280]{1,0:T(8,128)(2,1)S(1)} %collective-permute-done.1.after, bf16[128,1280]{1,0:T(8,128)(2,1)S(1)} %collective-permute-done.2.far0, ...), custom_call_target="tpu_custom_call" | custom-call | flops 1342177280 | bytes 8388608 | tf_op jit(solution)/shard_map/project/pallas_call | solution.py:191
  54.7 6.6 %collective-permute-done.12.refs_5_ = bf16[2,32,2048]{2,1,0:T(8,128)(2,1)} collective-permute-done((bf16[2,32,2048]{2,1,0:T(8,128)(2,1)}, bf16[2,32,2048]{2,1,0:T(8,128)(2,1)}, u32[]{:S(2)}, u32[]{:S(2)}) %collective-permute-start.12) | collective-permute-done | bytes 262176 | tf_op jit(solution)/shard_map/ppermute | solution.py:366
  61.3 0.9 collective-permute-start.4
  62.2 0.5 collective-permute-start.5
  62.8 11.4 %collective-permute-done.14.refs_7_ = bf16[2,32,2048]{2,1,0:T(8,128)(2,1)S(1)} collective-permute-done((bf16[2,32,2048]{2,1,0:T(8,128)(2,1)}, bf16[2,32,2048]{2,1,0:T(8,128)(2,1)S(1)}, u32[]{:S(2)}, u32[]{:S(2)}) %collective-permute-start.14) | collective-permute-done | bytes 262176 | tf_op jit(solution)/shard_map/ppermute | solution.py:366
  74.2 1.9 unpack.1.qt
  76.2 1.2 collective-permute-start.6
  77.4 0.6 collective-permute-start.7
  78.1 2.2 %collective-permute-done.6 = bf16[256,256]{1,0:T(8,128)(2,1)S(1)} collective-permute-done((bf16[256,256]{1,0:T(8,128)(2,1)S(1)}, bf16[256,256]{1,0:T(8,128)(2,1)S(1)}, u32[]{:S(2)}, u32[]{:S(2)}) %collective-permute-start.6) | collective-permute-done | bytes 131104 | tf_op jit(solution)/shard_map/ppermute | solution.py:352
  80.3 1.3 collective-permute-done.7
  81.6 4.1 %collective-permute-start.17 = (bf16[2048,256]{1,0:T(8,128)(2,1)S(1)}, bf16[2048,256]{1,0:T(8,128)(2,1)S(1)}, u32[]{:S(2)}, u32[]{:S(2)}) collective-permute-start(bf16[2048,256]{1,0:T(8,128)(2,1)S(1)} %constant_dynamic-update-slice_fusion), channel_id=1, source_target_pairs={{0,32},{32,0},{64,96},{96,64},{128,160},{160,128},{192,224},{224,1... | collective-permute-start | bytes 3145736 | tf_op jit(solution)/shard_map/ppermute | solution.py:358
  85.8 1.3 collective-permute-start.15
  87.0 0.2 collective-permute-start.16
  87.2 0.8 collective-permute-done.17
  88.1 15.0 %attend.5 = (f32[16,1,256]{2,1,0:T(1,128)S(1)}, f32[16,1,256]{2,1,0:T(1,128)S(1)}, f32[16,128,256]{2,1,0:T(8,128)S(1)}) custom-call(s32[1920]{0:T(1024)S(1)} %copy-done.10, s32[48]{0:T(128)S(1)} %copy-done.11, s32[8]{0:T(128)S(1)} %copy-done.6, bf16[8,2,128,256]{3,2,1,0:T(8,128)(2,1)S(1)} %unpack.1.qt, bf16[8,256,256]{2,1,0:T(8,128)(2,1)S(1)} %bitcast.23, ...), custom_call_target="tpu_custom_call" | custom-call | flops 2147483648 | bytes 6291456 | tf_op jit(solution)/shard_map/attend/pallas_call | solution.py:326
  103.0 7.5 %collective-permute-done.15 = bf16[2048,256]{1,0:T(8,128)(2,1)S(1)} collective-permute-done((bf16[2048,256]{1,0:T(8,128)(2,1)S(1)}, bf16[2048,256]{1,0:T(8,128)(2,1)S(1)}, u32[]{:S(2)}, u32[]{:S(2)}) %collective-permute-start.15) | collective-permute-done | bytes 1048608 | tf_op jit(solution)/shard_map/ppermute | solution.py:391
  110.5 1.8 collective-permute-done.16
  112.3 0.9 collective-permute-start.20
  113.1 0.0 collective-permute-start.21
  113.1 1.5 collective-permute-start.18
  114.6 0.8 collective-permute-done.20
  115.4 1.5 collective-permute-done.21
  116.9 18.6 %attend.6 = (f32[16,1,256]{2,1,0:T(1,128)S(1)}, f32[16,1,256]{2,1,0:T(1,128)S(1)}, f32[16,128,256]{2,1,0:T(8,128)S(1)}) custom-call(s32[1920]{0:T(1024)S(1)} %copy-done.10, s32[48]{0:T(128)S(1)} %copy-done.11, s32[8]{0:T(128)S(1)} %copy-done.6, bf16[8,2,128,256]{3,2,1,0:T(8,128)(2,1)S(1)} %unpack.1.qt, bf16[8,256,256]{2,1,0:T(8,128)(2,1)S(1)} %bitcast.26, ...), custom_call_target="tpu_custom_call" | custom-call | flops 2147483648 | bytes 6291456 | tf_op jit(solution)/shard_map/attend/pallas_call | solution.py:326
  135.5 1.8 collective-permute-done.18
  137.3 1.1 collective-permute-done.19
  138.5 1.7 collective-permute-start.24
  140.2 1.2 collective-permute-start.22
  141.4 0.3 collective-permute-start.23
  141.6 0.8 collective-permute-done.24
  142.5 1.5 collective-permute-done.25
  143.9 16.1 %attend.7 = (f32[16,1,256]{2,1,0:T(1,128)S(1)}, f32[16,1,256]{2,1,0:T(1,128)S(1)}, f32[16,128,256]{2,1,0:T(8,128)S(1)}) custom-call(s32[1920]{0:T(1024)S(1)} %copy-done.10, s32[48]{0:T(128)S(1)} %copy-done.11, s32[8]{0:T(128)S(1)} %copy-done.6, bf16[8,2,128,256]{3,2,1,0:T(8,128)(2,1)S(1)} %unpack.1.qt, bf16[8,256,256]{2,1,0:T(8,128)(2,1)S(1)} %bitcast.24, ...), custom_call_target="tpu_custom_call" | custom-call | flops 2147483648 | bytes 6291456 | tf_op jit(solution)/shard_map/attend/pallas_call | solution.py:326
  160.1 4.3 %collective-permute-done.22 = bf16[2048,256]{1,0:T(8,128)(2,1)S(1)} collective-permute-done((bf16[2048,256]{1,0:T(8,128)(2,1)S(1)}, bf16[2048,256]{1,0:T(8,128)(2,1)S(1)}, u32[]{:S(2)}, u32[]{:S(2)}) %collective-permute-start.22) | collective-permute-done | bytes 1048608 | tf_op jit(solution)/shard_map/ppermute | solution.py:391
  164.4 1.8 collective-permute-done.23
  166.2 1.4 collective-permute-start.28
  167.7 1.8 collective-permute-start.26
  169.4 0.4 collective-permute-done.28
  169.9 1.5 collective-permute-done.29
  171.4 17.8 %attend.8 = (f32[16,1,256]{2,1,0:T(1,128)S(1)}, f32[16,1,256]{2,1,0:T(1,128)S(1)}, f32[16,128,256]{2,1,0:T(8,128)S(1)}) custom-call(s32[1920]{0:T(1024)S(1)} %copy-done.10, s32[48]{0:T(128)S(1)} %copy-done.11, s32[8]{0:T(128)S(1)} %copy-done.6, bf16[8,2,128,256]{3,2,1,0:T(8,128)(2,1)S(1)} %unpack.1.qt, bf16[8,256,256]{2,1,0:T(8,128)(2,1)S(1)} %bitcast.21, ...), custom_call_target="tpu_custom_call" | custom-call | flops 2147483648 | bytes 6291456 | tf_op jit(solution)/shard_map/attend/pallas_call | solution.py:326
  189.2 0.1 collective-permute-start.30
  189.3 0.5 collective-permute-start.31
  189.8 1.4 collective-permute-done.30
  191.2 0.7 collective-permute-done.31
  191.9 13.5 %attend.9 = bf16[256,2048]{1,0:T(8,128)(2,1)} custom-call(s32[1920]{0:T(1024)S(1)} %copy-done.10, s32[48]{0:T(128)S(1)} %copy-done.11, s32[8]{0:T(128)S(1)} %copy-done.6, bf16[8,2,128,256]{3,2,1,0:T(8,128)(2,1)S(1)} %unpack.1.qt, bf16[4,256,256]{2,1,0:T(8,128)(2,1)S(1)} %bitcast.35, bf16[4,256,256]{2,1,0:T(8,128)(2,1)S(1)} %bitcast.36, ...), custom_call_target="tpu_custom_call" | custom-call | flops 2147483648 | bytes 6291456 | tf_op jit(solution)/shard_map/attend/pallas_call | solution.py:326
  (46 shorter events, 0.3 us)
Async XLA Ops:
  0.0 17.2 %collective-permute-start = (bf16[256,1280]{1,0:T(8,128)(2,1)}, bf16[256,1280]{1,0:T(8,128)(2,1)S(1)}, u32[]{:S(2)}, u32[]{:S(2)}) collective-permute-start(bf16[256,1280]{1,0:T(8,128)(2,1)} %own), channel_id=1, source_target_pairs={{0,1},{1,2},{2,3},{3,0},{4,5},{5,6},{6,7},{7,4},{8,9},{9,10},{10,1... | collective-permute-start | bytes 1966088 | tf_op jit(solution)/shard_map/ppermute | solution.py:349
  1.3 15.9 %collective-permute-start.1 = (bf16[256,1280]{1,0:T(8,128)(2,1)}, bf16[256,1280]{1,0:T(8,128)(2,1)S(1)}, u32[]{:S(2)}, u32[]{:S(2)}) collective-permute-start(bf16[256,1280]{1,0:T(8,128)(2,1)} %own), channel_id=1, source_target_pairs={{0,3},{1,0},{2,1},{3,2},{4,7},{5,4},{6,5},{7,6},{8,11},{9,8},{10,9... | collective-permute-start | bytes 1966088 | tf_op jit(solution)/shard_map/ppermute | solution.py:350
  2.8 1.2 copy-start.2
  4.0 0.7 copy-start.4
  4.7 44.4 %copy-start.3 = (bf16[256,1280]{1,0:T(8,128)(2,1)S(1)}, bf16[256,1280]{1,0:T(8,128)(2,1)}, u32[]{:S(2)}) copy-start(bf16[256,1280]{1,0:T(8,128)(2,1)} %own) | copy-start | bytes 1966084
  7.1 24.1 %copy-start.5 = (s32[8]{0:T(128)}, s32[8]{0:T(128)S(1)}, u32[]{:S(2)}) copy-start(s32[8]{0:T(128)S(1)} %get-tuple-element.72.info) | copy-start | bytes 100
  7.1 24.1 %copy-start.7 = (bf16[2,32,2048]{2,1,0:T(8,128)(2,1)}, bf16[2,32,2048]{2,1,0:T(8,128)(2,1)S(1)}, u32[]{:S(2)}) copy-start(bf16[2,32,2048]{2,1,0:T(8,128)(2,1)S(1)} %get-tuple-element.64) | copy-start | bytes 786436
  7.1 24.1 %copy-start.8 = (bf16[2,32,2048]{2,1,0:T(8,128)(2,1)}, bf16[2,32,2048]{2,1,0:T(8,128)(2,1)S(1)}, u32[]{:S(2)}) copy-start(bf16[2,32,2048]{2,1,0:T(8,128)(2,1)S(1)} %get-tuple-element.63) | copy-start | bytes 786436
  7.1 24.1 %copy-start.9 = (bf16[2,32,2048]{2,1,0:T(8,128)(2,1)}, bf16[2,32,2048]{2,1,0:T(8,128)(2,1)S(1)}, u32[]{:S(2)}) copy-start(bf16[2,32,2048]{2,1,0:T(8,128)(2,1)S(1)} %get-tuple-element.69) | copy-start | bytes 786436
  17.2 14.0 %collective-permute-start.2 = (bf16[128,1280]{1,0:T(8,128)(2,1)S(1)}, bf16[128,1280]{1,0:T(8,128)(2,1)S(1)}, u32[]{:S(2)}, u32[]{:S(2)}) collective-permute-start(bf16[128,1280]{1,0:T(8,128)(2,1)S(1)} %slice.18), channel_id=1, source_target_pairs={{0,1},{1,2},{2,3},{3,0},{4,5},{5,6},{6,7},{7,4},{8,9},{9,10},{10,1... | collective-permute-start | bytes 983048 | tf_op jit(solution)/shard_map/ppermute | solution.py:352
  18.9 18.7 %collective-permute-start.3 = (bf16[128,1280]{1,0:T(8,128)(2,1)}, bf16[128,1280]{1,0:T(8,128)(2,1)S(1)}, u32[]{:S(2)}, u32[]{:S(2)}) collective-permute-start(bf16[128,1280]{1,0:T(8,128)(2,1)} %slice.19), channel_id=1, source_target_pairs={{0,3},{1,0},{2,1},{3,2},{4,7},{5,4},{6,5},{7,6},{8,11},{9,8},{10,9... | collective-permute-start | bytes 983048 | tf_op jit(solution)/shard_map/ppermute | solution.py:353
  20.7 24.1 %collective-permute-start.10 = (bf16[2,32,2048]{2,1,0:T(8,128)(2,1)}, bf16[2,32,2048]{2,1,0:T(8,128)(2,1)S(1)}, u32[]{:S(2)}, u32[]{:S(2)}) collective-permute-start(bf16[2,32,2048]{2,1,0:T(8,128)(2,1)} %get-tuple-element.65), channel_id=1, source_target_pairs={{0,12},{4,16},{8,20},{12,24},{16,28},{20,0},{24,4},{28,8},{1,13},{... | collective-permute-start | bytes 786440 | tf_op jit(solution)/shard_map/ppermute | solution.py:366
  26.2 18.6 %collective-permute-start.11 = (bf16[2,32,2048]{2,1,0:T(8,128)(2,1)}, bf16[2,32,2048]{2,1,0:T(8,128)(2,1)S(1)}, u32[]{:S(2)}, u32[]{:S(2)}) collective-permute-start(bf16[2,32,2048]{2,1,0:T(8,128)(2,1)} %get-tuple-element.66), channel_id=1, source_target_pairs={{0,16},{4,20},{8,24},{12,28},{16,0},{20,4},{24,8},{28,12},{1,17},{... | collective-permute-start | bytes 786440 | tf_op jit(solution)/shard_map/ppermute | solution.py:366
  26.7 34.6 %collective-permute-start.12 = (bf16[2,32,2048]{2,1,0:T(8,128)(2,1)}, bf16[2,32,2048]{2,1,0:T(8,128)(2,1)}, u32[]{:S(2)}, u32[]{:S(2)}) collective-permute-start(bf16[2,32,2048]{2,1,0:T(8,128)(2,1)} %get-tuple-element.67), channel_id=1, source_target_pairs={{0,20},{4,24},{8,28},{12,0},{16,4},{20,8},{24,12},{28,16},{1,21},{... | collective-permute-start | bytes 786440 | tf_op jit(solution)/shard_map/ppermute | solution.py:366
  31.2 31.0 %collective-permute-start.13 = (bf16[2,32,2048]{2,1,0:T(8,128)(2,1)}, bf16[2,32,2048]{2,1,0:T(8,128)(2,1)}, u32[]{:S(2)}, u32[]{:S(2)}) collective-permute-start(bf16[2,32,2048]{2,1,0:T(8,128)(2,1)} %get-tuple-element.68), channel_id=1, source_target_pairs={{0,24},{4,28},{8,0},{12,4},{16,8},{20,12},{24,16},{28,20},{1,25},{... | collective-permute-start | bytes 786440 | tf_op jit(solution)/shard_map/ppermute | solution.py:366
  37.7 36.6 %collective-permute-start.14 = (bf16[2,32,2048]{2,1,0:T(8,128)(2,1)}, bf16[2,32,2048]{2,1,0:T(8,128)(2,1)S(1)}, u32[]{:S(2)}, u32[]{:S(2)}) collective-permute-start(bf16[2,32,2048]{2,1,0:T(8,128)(2,1)} %copy-done.9), channel_id=1, source_target_pairs={{0,28},{4,0},{8,4},{12,8},{16,12},{20,16},{24,20},{28,24},{1,29},{... | collective-permute-start | bytes 786440 | tf_op jit(solution)/shard_map/ppermute | solution.py:366
  44.8 29.4 %collective-permute-start.8 = (bf16[2,32,2048]{2,1,0:T(8,128)(2,1)}, bf16[2,32,2048]{2,1,0:T(8,128)(2,1)S(1)}, u32[]{:S(2)}, u32[]{:S(2)}) collective-permute-start(bf16[2,32,2048]{2,1,0:T(8,128)(2,1)} %copy-done.8), channel_id=1, source_target_pairs={{0,4},{4,8},{8,12},{12,16},{16,20},{20,24},{24,28},{28,0},{1,5},{5... | collective-permute-start | bytes 786440 | tf_op jit(solution)/shard_map/ppermute | solution.py:366
  44.8 29.4 %collective-permute-start.9 = (bf16[2,32,2048]{2,1,0:T(8,128)(2,1)}, bf16[2,32,2048]{2,1,0:T(8,128)(2,1)S(1)}, u32[]{:S(2)}, u32[]{:S(2)}) collective-permute-start(bf16[2,32,2048]{2,1,0:T(8,128)(2,1)} %copy-done.7), channel_id=1, source_target_pairs={{0,8},{4,12},{8,16},{12,20},{16,24},{20,28},{24,0},{28,4},{1,9},{5... | collective-permute-start | bytes 786440 | tf_op jit(solution)/shard_map/ppermute | solution.py:366
  49.1 1.7 copy-start
  50.8 1.7 copy-start.1
  61.3 14.9 %collective-permute-start.4 = (bf16[512,256]{1,0:T(8,128)(2,1)S(1)}, bf16[512,256]{1,0:T(8,128)(2,1)S(1)}, u32[]{:S(2)}, u32[]{:S(2)}) collective-permute-start(bf16[512,256]{1,0:T(8,128)(2,1)S(1)} %project.1), channel_id=1, source_target_pairs={{0,64},{32,96},{64,128},{96,160},{128,192},{160,224},{192,0},{224,... | collective-permute-start | bytes 786440 | tf_op jit(solution)/shard_map/ppermute | solution.py:349
  62.2 14.0 %collective-permute-start.5 = (bf16[512,256]{1,0:T(8,128)(2,1)S(1)}, bf16[512,256]{1,0:T(8,128)(2,1)S(1)}, u32[]{:S(2)}, u32[]{:S(2)}) collective-permute-start(bf16[512,256]{1,0:T(8,128)(2,1)S(1)} %project.1), channel_id=1, source_target_pairs={{0,192},{32,224},{64,0},{96,32},{128,64},{160,96},{192,128},{224,1... | collective-permute-start | bytes 786440 | tf_op jit(solution)/shard_map/ppermute | solution.py:350
  76.1 11.9 %copy-start.6 = (s32[8]{0:T(128)S(1)}, s32[8]{0:T(128)}, u32[]{:S(2)}) copy-start(s32[8]{0:T(128)} %copy-done.5) | copy-start | bytes 100
  76.1 11.9 %copy-start.10 = (s32[1920]{0:T(1024)S(1)}, s32[1920]{0:T(1024)}, u32[]{:S(2)}) copy-start(s32[1920]{0:T(1024)} %get-tuple-element.75.lists) | copy-start | bytes 23044
  76.2 11.9 %copy-start.11 = (s32[48]{0:T(128)S(1)}, s32[48]{0:T(128)}, u32[]{:S(2)}) copy-start(s32[48]{0:T(128)} %get-tuple-element.76.counts) | copy-start | bytes 580
  76.2 4.1 %collective-permute-start.6 = (bf16[256,256]{1,0:T(8,128)(2,1)S(1)}, bf16[256,256]{1,0:T(8,128)(2,1)S(1)}, u32[]{:S(2)}, u32[]{:S(2)}) collective-permute-start(bf16[256,256]{1,0:T(8,128)(2,1)S(1)} %slice.20), channel_id=1, source_target_pairs={{0,64},{32,96},{64,128},{96,160},{128,192},{160,224},{192,0},{224,... | collective-permute-start | bytes 393224 | tf_op jit(solution)/shard_map/ppermute | solution.py:352
  77.4 4.2 %collective-permute-start.7 = (bf16[256,256]{1,0:T(8,128)(2,1)S(1)}, bf16[256,256]{1,0:T(8,128)(2,1)S(1)}, u32[]{:S(2)}, u32[]{:S(2)}) collective-permute-start(bf16[256,256]{1,0:T(8,128)(2,1)S(1)} %slice.21), channel_id=1, source_target_pairs={{0,192},{32,224},{64,0},{96,32},{128,64},{160,96},{192,128},{224,1... | collective-permute-start | bytes 393224 | tf_op jit(solution)/shard_map/ppermute | solution.py:353
  81.6 6.4 %collective-permute-start.17 = (bf16[2048,256]{1,0:T(8,128)(2,1)S(1)}, bf16[2048,256]{1,0:T(8,128)(2,1)S(1)}, u32[]{:S(2)}, u32[]{:S(2)}) collective-permute-start(bf16[2048,256]{1,0:T(8,128)(2,1)S(1)} %constant_dynamic-update-slice_fusion), channel_id=1, source_target_pairs={{0,32},{32,0},{64,96},{96,64},{128,160},{160,128},{192,224},{224,1... | collective-permute-start | bytes 3145736 | tf_op jit(solution)/shard_map/ppermute | solution.py:358
  85.8 24.7 %collective-permute-start.15 = (bf16[2048,256]{1,0:T(8,128)(2,1)S(1)}, bf16[2048,256]{1,0:T(8,128)(2,1)S(1)}, u32[]{:S(2)}, u32[]{:S(2)}) collective-permute-start(bf16[2048,256]{1,0:T(8,128)(2,1)S(1)} %constant_dynamic-update-slice_fusion), channel_id=1, source_target_pairs={{0,4},{4,8},{8,12},{12,16},{16,20},{20,24},{24,28},{28,0},{1,5},{5... | collective-permute-start | bytes 3145736 | tf_op jit(solution)/shard_map/ppermute | solution.py:391
  87.0 25.2 %collective-permute-start.16 = (bf16[2048,256]{1,0:T(8,128)(2,1)S(1)}, bf16[2048,256]{1,0:T(8,128)(2,1)S(1)}, u32[]{:S(2)}, u32[]{:S(2)}) collective-permute-start(bf16[2048,256]{1,0:T(8,128)(2,1)S(1)} %constant_dynamic-update-slice_fusion), channel_id=1, source_target_pairs={{0,28},{4,0},{8,4},{12,8},{16,12},{20,16},{24,20},{28,24},{1,29},{... | collective-permute-start | bytes 3145736 | tf_op jit(solution)/shard_map/ppermute | solution.py:391
  112.3 3.2 %collective-permute-start.20 = (bf16[2048,256]{1,0:T(8,128)(2,1)S(1)}, bf16[2048,256]{1,0:T(8,128)(2,1)S(1)}, u32[]{:S(2)}, u32[]{:S(2)}) collective-permute-start(bf16[2048,256]{1,0:T(8,128)(2,1)S(1)} %collective-permute-done.15), channel_id=1, source_target_pairs={{0,32},{32,0},{64,96},{96,64},{128,160},{160,128},{192,224},{224,1... | collective-permute-start | bytes 3145736 | tf_op jit(solution)/shard_map/ppermute | solution.py:358
  113.1 3.8 %collective-permute-start.21 = (bf16[2048,256]{1,0:T(8,128)(2,1)S(1)}, bf16[2048,256]{1,0:T(8,128)(2,1)S(1)}, u32[]{:S(2)}, u32[]{:S(2)}) collective-permute-start(bf16[2048,256]{1,0:T(8,128)(2,1)S(1)} %collective-permute-done.16), channel_id=1, source_target_pairs={{0,32},{32,0},{64,96},{96,64},{128,160},{160,128},{192,224},{224,1... | collective-permute-start | bytes 3145736 | tf_op jit(solution)/shard_map/ppermute | solution.py:358
  113.1 24.2 %collective-permute-start.18 = (bf16[2048,256]{1,0:T(8,128)(2,1)S(1)}, bf16[2048,256]{1,0:T(8,128)(2,1)S(1)}, u32[]{:S(2)}, u32[]{:S(2)}) collective-permute-start(bf16[2048,256]{1,0:T(8,128)(2,1)S(1)} %collective-permute-done.15), channel_id=1, source_target_pairs={{0,4},{4,8},{8,12},{12,16},{16,20},{20,24},{24,28},{28,0},{1,5},{5... | collective-permute-start | bytes 3145736 | tf_op jit(solution)/shard_map/ppermute | solution.py:391
  114.6 23.9 %collective-permute-start.19 = (bf16[2048,256]{1,0:T(8,128)(2,1)S(1)}, bf16[2048,256]{1,0:T(8,128)(2,1)S(1)}, u32[]{:S(2)}, u32[]{:S(2)}) collective-permute-start(bf16[2048,256]{1,0:T(8,128)(2,1)S(1)} %collective-permute-done.16), channel_id=1, source_target_pairs={{0,28},{4,0},{8,4},{12,8},{16,12},{20,16},{24,20},{28,24},{1,29},{... | collective-permute-start | bytes 3145736 | tf_op jit(solution)/shard_map/ppermute | solution.py:391
  138.5 4.0 %collective-permute-start.24 = (bf16[2048,256]{1,0:T(8,128)(2,1)S(1)}, bf16[2048,256]{1,0:T(8,128)(2,1)S(1)}, u32[]{:S(2)}, u32[]{:S(2)}) collective-permute-start(bf16[2048,256]{1,0:T(8,128)(2,1)S(1)} %collective-permute-done.18), channel_id=1, source_target_pairs={{0,32},{32,0},{64,96},{96,64},{128,160},{160,128},{192,224},{224,1... | collective-permute-start | bytes 3145736 | tf_op jit(solution)/shard_map/ppermute | solution.py:358
  140.2 3.8 %collective-permute-start.25 = (bf16[2048,256]{1,0:T(8,128)(2,1)S(1)}, bf16[2048,256]{1,0:T(8,128)(2,1)S(1)}, u32[]{:S(2)}, u32[]{:S(2)}) collective-permute-start(bf16[2048,256]{1,0:T(8,128)(2,1)S(1)} %collective-permute-done.19), channel_id=1, source_target_pairs={{0,32},{32,0},{64,96},{96,64},{128,160},{160,128},{192,224},{224,1... | collective-permute-start | bytes 3145736 | tf_op jit(solution)/shard_map/ppermute | solution.py:358
  140.2 24.2 %collective-permute-start.22 = (bf16[2048,256]{1,0:T(8,128)(2,1)S(1)}, bf16[2048,256]{1,0:T(8,128)(2,1)S(1)}, u32[]{:S(2)}, u32[]{:S(2)}) collective-permute-start(bf16[2048,256]{1,0:T(8,128)(2,1)S(1)} %collective-permute-done.18), channel_id=1, source_target_pairs={{0,4},{4,8},{8,12},{12,16},{16,20},{20,24},{24,28},{28,0},{1,5},{5... | collective-permute-start | bytes 3145736 | tf_op jit(solution)/shard_map/ppermute | solution.py:391
  141.4 24.8 %collective-permute-start.23 = (bf16[2048,256]{1,0:T(8,128)(2,1)S(1)}, bf16[2048,256]{1,0:T(8,128)(2,1)S(1)}, u32[]{:S(2)}, u32[]{:S(2)}) collective-permute-start(bf16[2048,256]{1,0:T(8,128)(2,1)S(1)} %collective-permute-done.19), channel_id=1, source_target_pairs={{0,28},{4,0},{8,4},{12,8},{16,12},{20,16},{24,20},{28,24},{1,29},{... | collective-permute-start | bytes 3145736 | tf_op jit(solution)/shard_map/ppermute | solution.py:391
  166.2 3.6 %collective-permute-start.28 = (bf16[2048,256]{1,0:T(8,128)(2,1)S(1)}, bf16[2048,256]{1,0:T(8,128)(2,1)S(1)}, u32[]{:S(2)}, u32[]{:S(2)}) collective-permute-start(bf16[2048,256]{1,0:T(8,128)(2,1)S(1)} %collective-permute-done.22), channel_id=1, source_target_pairs={{0,32},{32,0},{64,96},{96,64},{128,160},{160,128},{192,224},{224,1... | collective-permute-start | bytes 3145736 | tf_op jit(solution)/shard_map/ppermute | solution.py:358
  167.6 3.8 %collective-permute-start.29 = (bf16[2048,256]{1,0:T(8,128)(2,1)S(1)}, bf16[2048,256]{1,0:T(8,128)(2,1)S(1)}, u32[]{:S(2)}, u32[]{:S(2)}) collective-permute-start(bf16[2048,256]{1,0:T(8,128)(2,1)S(1)} %collective-permute-done.23), channel_id=1, source_target_pairs={{0,32},{32,0},{64,96},{96,64},{128,160},{160,128},{192,224},{224,1... | collective-permute-start | bytes 3145736 | tf_op jit(solution)/shard_map/ppermute | solution.py:358
  167.7 21.5 %collective-permute-start.26 = (bf16[1024,256]{1,0:T(8,128)(2,1)S(1)}, bf16[1024,256]{1,0:T(8,128)(2,1)S(1)}, u32[]{:S(2)}, u32[]{:S(2)}) collective-permute-start(bf16[1024,256]{1,0:T(8,128)(2,1)S(1)} %slice.22), channel_id=1, source_target_pairs={{0,4},{4,8},{8,12},{12,16},{16,20},{20,24},{24,28},{28,0},{1,5},{5... | collective-permute-start | bytes 1572872 | tf_op jit(solution)/shard_map/ppermute | solution.py:393
  169.4 19.7 %collective-permute-start.27 = (bf16[1024,256]{1,0:T(8,128)(2,1)S(1)}, bf16[1024,256]{1,0:T(8,128)(2,1)S(1)}, u32[]{:S(2)}, u32[]{:S(2)}) collective-permute-start(bf16[1024,256]{1,0:T(8,128)(2,1)S(1)} %slice.23), channel_id=1, source_target_pairs={{0,28},{4,0},{8,4},{12,8},{16,12},{20,16},{24,20},{28,24},{1,29},{... | collective-permute-start | bytes 1572872 | tf_op jit(solution)/shard_map/ppermute | solution.py:393
  189.2 2.0 collective-permute-start.30
  189.3 2.6 %collective-permute-start.31 = (bf16[1024,256]{1,0:T(8,128)(2,1)S(1)}, bf16[1024,256]{1,0:T(8,128)(2,1)S(1)}, u32[]{:S(2)}, u32[]{:S(2)}) collective-permute-start(bf16[1024,256]{1,0:T(8,128)(2,1)S(1)} %collective-permute-done.27), channel_id=1, source_target_pairs={{0,32},{32,0},{64,96},{96,64},{128,160},{160,128},{192,224},{224,1... | collective-permute-start | bytes 1572872 | tf_op jit(solution)/shard_map/ppermute | solution.py:358
where the time goes:
time: 208 us; the launch traced here: 206 us
  Pallas kernels  93 us (45%)
  waiting for transfers between devices  66 us (32%)
  starting transfers between devices  39.2 us (19%)
  local copies, waits for them, and re-layouts  6.35 us (3%)
    pallas_call x5, Pallas kernels, attend(): pl.pallas_call(functools.partial(attend_kernel, which, len(pieces)), in_s...  81 us
    ppermute x7, waiting for transfers between devices, on_device(): lax.ppermute(sends[s], 'ctx', turn(NZ, s))  24.6 us
    ppermute x6, waiting for transfers between devices, on_device(): low, high = (lax.ppermute(low, 'ctx', ZP), lax.ppermute(high, 'ctx', ZM))  18.3 us
    ppermute x7, starting transfers between devices, on_device(): lax.ppermute(sends[s], 'ctx', turn(NZ, s))  15.6 us
    ppermute x2, waiting for transfers between devices, ring_four(): low = lax.ppermute(block, axis, up)  10 us
    ppermute x9, waiting for transfers between devices, swapped(): pieces = pieces + [lax.ppermute(a, 'leaf', CS) for a in pieces]  9.52 us
    ppermute x9, starting transfers between devices, swapped(): pieces = pieces + [lax.ppermute(a, 'leaf', CS) for a in pieces]  8.62 us
    pallas_call x1, Pallas kernels, walk(): pl.pallas_call(walk_kernel, in_specs=[smem()] * 4, out_specs=[smem()] * 2...  5.65 us
  transfers between devices with their start and end apart: 32, of which 21 were waited for; matrix products, arithmetic and copies ran while one was open for 1% of the time, Pallas kernels for 39%

commit v1 on v0

v1 whole, which is shorter than its diff:
```python
import functools
import math

import jax
import jax.numpy as jnp
from jax import lax
from jax.experimental import pallas as pl
from jax.experimental.pallas import tpu as pltpu
from jax.sharding import PartitionSpec as P

HEAD = 128
GROUP = 8
SEG = 128
TILE = 32
TPD = 8
CAP = 2
NX, NZ, NY = 4, 8, 4
ROWS = TILE * GROUP
SCALE = math.log2(math.e) / math.sqrt(HEAD)
FILL = -1.2e31
MIB = 1 << 20
UNIT = 4
PASSES = 5
ITEMS = 8 * 32 // UNIT + 4

XP = [(2 * x + c, 2 * ((x + 1) % NX) + c) for x in range(NX) for c in range(2)]
XM = [(2 * x + c, 2 * ((x - 1) % NX) + c) for x in range(NX) for c in range(2)]
CS = [(i, i ^ 1) for i in range(2 * NX)]


def turn(n, by):
    return [(i, (i + by) % n) for i in range(n)]


ZP, ZM = turn(NZ, 1), turn(NZ, -1)
YP, YM = turn(NY, 1), turn(NY, -1)

smem = functools.partial(pl.BlockSpec, memory_space=pltpu.SMEM)
vmem = functools.partial(pl.BlockSpec, memory_space=pltpu.VMEM)


def pack_kernel(where, dest, q, *outs):
    sends, table, info = outs[:NZ], outs[NZ], outs[NZ + 1]
    leaf, ctx = where[0], where[1]
    device = leaf * NZ + ctx
    shifts = [((dest[device * TPD + j] >> 3) - ctx) & (NZ - 1) for j in range(TPD)]
    ranks = []
    for j in range(TPD):
        rank = jnp.int32(0)
        for i in range(j):
            rank = rank + (shifts[i] == shifts[j]).astype(jnp.int32)
        ranks.append(rank)
    for s in range(NZ):
        for r in range(CAP):
            pick = jnp.int32(0)
            for j in range(TPD):
                pick = jnp.where((shifts[j] == s) & (ranks[j] == r), j, pick)
            sends[s][r] = q[pl.ds(pl.multiple_of(pick * TILE, TILE), TILE), :]
    for s in range(NZ):
        base = (leaf * NZ + ((ctx - s) & (NZ - 1))) * TPD
        table[s * CAP] = jnp.int32(-1)
        table[s * CAP + 1] = jnp.int32(-1)

        def one(j, rank, s=s, base=base):
            to = dest[base + j]
            mine = (to >> 3) == device

            @pl.when(mine)
            def _():
                table[s * CAP + rank] = to & (TPD - 1)
                info[to & (TPD - 1)] = base + j

            return rank + mine.astype(jnp.int32)

        lax.fori_loop(0, TPD, one, jnp.int32(0))


def pack(where, dest, q):
    width = q.shape[1]
    outs = pl.pallas_call(
        pack_kernel,
        in_specs=[smem(), smem(), vmem()],
        out_specs=[vmem()] * NZ + [smem(), smem()],
        out_shape=[jax.ShapeDtypeStruct((CAP, TILE, width), q.dtype)] * NZ
        + [jax.ShapeDtypeStruct((NZ * CAP,), jnp.int32), jax.ShapeDtypeStruct((TPD,), jnp.int32)],
        compiler_params=pltpu.CompilerParams(vmem_limit_bytes=32 * MIB),
        cost_estimate=pl.CostEstimate(flops=0, bytes_accessed=3 * MIB, transcendentals=0),
        name="pack",
    )(where, dest, q)
    return outs[:NZ], outs[NZ], outs[NZ + 1]


def walk_kernel(parents, info, which, place, lists, tiles, counts):
    for p in range(PASSES):
        counts[p] = jnp.int32(0)

    def tile(d, carry):
        seg = info[d] >> 2

        def body(at):
            p = which[at]
            used = counts[p]

            @pl.when((used & (UNIT - 1)) == 0)
            def _():
                tiles[p * ITEMS + used // UNIT] = d + jnp.where(at == seg, TPD, 0)

            lists[p * ITEMS * UNIT + used] = place[at]
            counts[p] = used + 1
            return parents[at]

        lax.while_loop(lambda at: at >= 0, body, seg)
        for p in range(PASSES):
            used = counts[p]
            for n in range(UNIT):
                lists[p * ITEMS * UNIT + used + n] = jnp.int32(-1)
            counts[p] = ((used + UNIT - 1) // UNIT) * UNIT
        return carry

    lax.fori_loop(0, TPD, tile, 0)
    for p in range(PASSES):
        used = counts[p]
        tiles[p * ITEMS + used // UNIT] = jnp.int32(0)
        for n in range(UNIT):
            lists[p * ITEMS * UNIT + used + n] = jnp.int32(-1)


def walk(parents, info, which, place):
    return pl.pallas_call(
        walk_kernel,
        in_specs=[smem()] * 4,
        out_specs=[smem()] * 3,
        out_shape=[
            jax.ShapeDtypeStruct((PASSES * ITEMS * UNIT,), jnp.int32),
            jax.ShapeDtypeStruct((PASSES * ITEMS,), jnp.int32),
            jax.ShapeDtypeStruct((PASSES,), jnp.int32),
        ],
        cost_estimate=pl.CostEstimate(flops=0, bytes_accessed=16 * MIB, transcendentals=0),
        name="walk",
    )(parents, info, which, place)


def unpack_kernel(table, *refs):
    came, out = refs[:NZ], refs[NZ]
    for s in range(NZ):

        def one(r, carry, s=s):
            d = table[s * CAP + r]

            @pl.when(d >= 0)
            def _():
                for g in range(2):
                    heads = [
                        came[s][r, :, pl.ds((g * GROUP + h) * HEAD, HEAD)] for h in range(GROUP)
                    ]
                    out[d, g] = jnp.concatenate(heads, axis=0).T

            return carry

        lax.fori_loop(0, CAP, one, 0)


def unpack(table, came):
    return pl.pallas_call(
        unpack_kernel,
        in_specs=[smem()] + [vmem()] * NZ,
        out_specs=vmem(),
        out_shape=jax.ShapeDtypeStruct((TPD, 2, HEAD, ROWS), jnp.bfloat16),
        compiler_params=pltpu.CompilerParams(vmem_limit_bytes=32 * MIB),
        cost_estimate=pl.CostEstimate(flops=0, bytes_accessed=6 * MIB, transcendentals=0),
        name="unpack",
    )(table, *came)


def project_kernel(where, own, before, after, far0, far1, wk, wv, out):
    y = where[2]
    depth = own.shape[1]
    half = far0.shape[0]

    def rows(by):
        at = (y + by) & (NY - 1)
        return pl.ds(pl.multiple_of(at * depth, depth), depth)

    def times(w):
        total = jnp.dot(own[...], w[rows(0), :], preferred_element_type=jnp.float32)
        total += jnp.dot(before[...], w[rows(NY - 1), :], preferred_element_type=jnp.float32)
        total += jnp.dot(after[...], w[rows(1), :], preferred_element_type=jnp.float32)
        far = jnp.concatenate([far0[...], far1[...]], axis=0)
        return total + jnp.dot(far, w[rows(2), :], preferred_element_type=jnp.float32)

    k = times(wk)
    v = times(wv)
    for n in range(2):
        at = n * 2 * SEG
        out[at : at + SEG, :] = k[n * SEG : (n + 1) * SEG].astype(out.dtype)
        for g in range(2):
            part = v[n * SEG : (n + 1) * SEG, g * HEAD : (g + 1) * HEAD]
            out[at + SEG : at + 2 * SEG, g * HEAD : (g + 1) * HEAD] = part.T.astype(out.dtype)


def project(where, own, before, after, far0, far1, wk, wv):
    return pl.pallas_call(
        project_kernel,
        in_specs=[smem()] + [vmem()] * 7,
        out_specs=vmem(),
        out_shape=jax.ShapeDtypeStruct((4 * SEG, 2 * HEAD), jnp.bfloat16),
        compiler_params=pltpu.CompilerParams(vmem_limit_bytes=40 * MIB),
        cost_estimate=pl.CostEstimate(flops=2 * 256 * 5120 * 512, bytes_accessed=8 * MIB, transcendentals=0),
        name="project",
    )(where, own, before, after, far0, far1, wk, wv)


def attend_kernel(which, n_pieces, lists, tiles, counts, info, qt, *refs):
    pieces, refs = refs[:n_pieces], refs[n_pieces:]
    first, finish = which == 0, which == PASSES - 1
    if not first:
        refs = refs[3:]
    top, total, acc = refs[:3]
    if finish:
        out, kv, score, peak, weight, sems = refs[3:]
    else:
        kv, score, peak, weight, sems = refs[3:]
    copies, at = [], 0
    for n, piece in enumerate(pieces):
        size = piece.shape[0]
        copies.append(pltpu.make_async_copy(piece, kv.at[pl.ds(at, size)], sems.at[n]))
        at += size
    for copy in copies:
        copy.start()
    if first:
        top[...] = jnp.full(top.shape, FILL, jnp.float32)
        total[...] = jnp.zeros(total.shape, jnp.float32)
        acc[...] = jnp.zeros(acc.shape, jnp.float32)
    weight[...] = jnp.zeros(weight.shape, weight.dtype)
    for copy in copies:
        copy.wait()

    def entries(j):
        return [lists[(which * ITEMS + j) * UNIT + u] for u in range(UNIT)]

    def places(j):
        return [jnp.maximum(e, 0) for e in entries(j)]

    def tile_of(j):
        return tiles[which * ITEMS + j] & (TPD - 1)

    def scores(j):
        d, spots = tile_of(j), places(j)
        for g in range(2):
            k = jnp.concatenate([kv[w, 0:SEG, g * HEAD : (g + 1) * HEAD] for w in spots], axis=0)
            s = jnp.dot(k, qt[d, g], preferred_element_type=jnp.float32)
            score[g] = s
            for u in range(UNIT):
                part = s[u * SEG : (u + 1) * SEG].reshape(SEG // 8, 8, ROWS)
                peak[g, u] = jnp.max(part, axis=0)

        @pl.when(tiles[which * ITEMS + j] >= TPD)
        def _():
            key = lax.broadcasted_iota(jnp.int32, (SEG, ROWS), 0)
            token = lax.broadcasted_iota(jnp.int32, (SEG, ROWS), 1) & (TILE - 1)
            ok = key <= token + (info[d] & 3) * TILE
            for g in range(2):
                s = jnp.where(ok, score[g, 0:SEG], FILL)
                score[g, 0:SEG] = s
                peak[g, 0] = jnp.max(s.reshape(SEG // 8, 8, ROWS), axis=0)

    def add(j, drops):
        d, spots = tile_of(j), places(j)
        for g in range(2):
            v = jnp.concatenate(
                [kv[w, SEG : 2 * SEG, g * HEAD : (g + 1) * HEAD] for w in spots], axis=1
            )
            acc[d * 2 + g] = acc[d * 2 + g] * drops[g] + jnp.dot(
                v, weight[g], preferred_element_type=jnp.float32
            )

    def body(j, drops):
        add(jnp.maximum(j - 1, 0), drops)
        d = tile_of(j)
        pens = [jnp.where(e < 0, 3e31, 0.0) for e in entries(j)]
        result = []
        for g in range(2):
            i = d * 2 + g
            old = top[i]
            peaks = functools.reduce(jnp.maximum, [peak[g, u] - pens[u] for u in range(UNIT)])
            new = jnp.maximum(old, jnp.max(peaks, axis=0, keepdims=True))
            drop = jnp.exp2((old - new) * SCALE)
            part = jnp.zeros((8, ROWS), jnp.float32)
            for u in range(UNIT):
                e = jnp.exp2((score[g, u * SEG : (u + 1) * SEG] - (new + pens[u])) * SCALE)
                part += jnp.sum(e.reshape(SEG // 8, 8, ROWS), axis=0)
                weight[g, u * SEG : (u + 1) * SEG] = e.astype(jnp.bfloat16)
            total[i] = total[i] * drop + jnp.sum(part, axis=0, keepdims=True)
            top[i] = new
            result.append(drop)
        scores(j + 1)
        return tuple(result)

    rounds = counts[which] // UNIT
    ones = jnp.ones((1, ROWS), jnp.float32)
    scores(0)
    drops = lax.fori_loop(0, rounds, body, (ones, ones))
    add(jnp.maximum(rounds - 1, 0), drops)

    if finish:

        def write(d, carry):
            for g in range(2):
                i = d * 2 + g
                o = (acc[i] / total[i]).T.astype(out.dtype)
                for h in range(GROUP):
                    out[
                        pl.ds(pl.multiple_of(d * TILE, TILE), TILE),
                        (g * GROUP + h) * HEAD : (g * GROUP + h + 1) * HEAD,
                    ] = o[h * TILE : (h + 1) * TILE]
            return carry

        lax.fori_loop(0, TPD, write, 0)


def attend(which, work, qt, pieces, state):
    first, finish = which == 0, which == PASSES - 1
    shapes = [
        jax.ShapeDtypeStruct((2 * TPD, 1, ROWS), jnp.float32),
        jax.ShapeDtypeStruct((2 * TPD, 1, ROWS), jnp.float32),
        jax.ShapeDtypeStruct((2 * TPD, HEAD, ROWS), jnp.float32),
    ]
    if finish:
        shapes.append(jax.ShapeDtypeStruct((TPD * TILE, 2 * GROUP * HEAD), jnp.bfloat16))
    blocks = sum(piece.shape[0] for piece in pieces)
    begin = len(work) + 1 + len(pieces)
    return pl.pallas_call(
        functools.partial(attend_kernel, which, len(pieces)),
        in_specs=[smem()] * len(work)
        + [vmem()]
        + [pl.BlockSpec(memory_space=pl.ANY)] * len(pieces)
        + [vmem()] * (0 if first else 3),
        out_specs=[vmem()] * len(shapes),
        out_shape=shapes,
        input_output_aliases={} if first else {begin + n: n for n in range(3)},
        scratch_shapes=[
            pltpu.VMEM((blocks, 2 * SEG, 2 * HEAD), jnp.bfloat16),
            pltpu.VMEM((2, UNIT * SEG, ROWS), jnp.float32),
            pltpu.VMEM((2, UNIT, 8, ROWS), jnp.float32),
            pltpu.VMEM((2, UNIT * SEG, ROWS), jnp.bfloat16),
            pltpu.SemaphoreType.DMA((len(pieces),)),
        ],
        compiler_params=pltpu.CompilerParams(vmem_limit_bytes=28 * MIB),
        cost_estimate=pl.CostEstimate(
            flops=256 * 16 * 128 * 128 * 32, bytes_accessed=6 * MIB, transcendentals=0
        ),
        name="attend",
    )(*work, qt, *pieces, *(() if first else state))


def cat(*parts):
    return jnp.concatenate(parts, axis=0)


def ring_four(block, axis, up, down, ready=()):
    half = block.shape[0] // 2
    low = lax.ppermute(block, axis, up)
    high = lax.ppermute(block, axis, down)
    low, high, _ = lax.optimization_barrier((low, high, ready))
    far0 = lax.ppermute(low[:half], axis, up)
    far1 = lax.ppermute(high[half:], axis, down)
    return [block, low, high, far0, far1]


def ring_z(block):
    half = block.shape[0] // 2
    parts = [block]
    low = high = block
    for _ in range(3):
        low = lax.ppermute(low, "ctx", ZP)
        high = lax.ppermute(high, "ctx", ZM)
        parts += [low, high]
    return parts + [lax.ppermute(low[:half], "ctx", ZP), lax.ppermute(high[half:], "ctx", ZM)]


def swapped(*pieces):
    pieces = list(pieces) + [lax.ppermute(a, "leaf", CS) for a in pieces]
    return [a.reshape(-1, 2 * SEG, 2 * HEAD) for a in pieces]


def on_device(queries, inputs, key_weight, value_weight, parents, tile_dest):
    leaf, ctx, y = lax.axis_index("leaf"), lax.axis_index("ctx"), lax.axis_index("head")
    where = jnp.stack([leaf, ctx, y]).astype(jnp.int32)
    sends, table, info = pack(where, tile_dest, queries)
    came = [sends[0]] + [lax.ppermute(sends[s], "ctx", turn(NZ, s)) for s in range(1, NZ)]
    rows = ring_four(inputs, "head", YP, YM, sends)

    seg = jnp.arange(parents.shape[0], dtype=jnp.int32)
    odd = (seg & 1) == 1
    block = seg >> 1
    from_leaf, from_z = block >> 3, block & (NZ - 1)
    z = (from_z - ctx) & (NZ - 1)
    x = ((from_leaf >> 1) - (leaf >> 1)) & (NX - 1)
    at_z = jnp.where(z == 0, 0, jnp.where(z < 4, 2 * z, jnp.where(z == 4, 7, 2 * (NZ - z) - 1)))
    at_x = jnp.where(x == 0, 0, jnp.where(x == 1, 2, jnp.where(x == 2, 3, 1)))
    which = jnp.where(
        odd,
        jnp.where(z <= 4, z, NZ - z),
        jnp.where(x == 0, 0, jnp.where(x == 3, 2, jnp.where(x == 1, 3, 4))),
    )
    ahead = jnp.where(odd & (z > 0) & (z < 4), 4, 0)
    start_odd = jnp.where(which == 0, 8, ahead)
    start_even = jnp.where(which == 0, 0, jnp.where(which == 4, 4, 8))
    place = jnp.where(odd, start_odd + at_x, start_even + at_z)
    span = jnp.where((which == 0) | (which == 4), 12, jnp.where(which == 1, 8, 16))
    place = place + span * ((from_leaf ^ leaf) & 1)
    work = list(walk(parents, info, which, place))
    rows, work, early = lax.optimization_barrier((rows, work, came[1:4] + came[5:]))
    came = [came[0]] + early[:3] + [came[4]] + early[3:]
    work.append(info)

    kv = project(where, *rows, key_weight, value_weight)
    half = kv.shape[0] // 2
    odds = cat(*ring_four(kv[half:], "leaf", XP, XM))
    evens = cat(*ring_z(kv[:half]))
    qt = unpack(table, came)
    odds, evens, qt = lax.optimization_barrier((odds, evens, qt))

    def along_z(a, b):
        return lax.ppermute(a, "ctx", ZP), lax.ppermute(b, "ctx", ZM)

    low, high = along_z(odds, odds)
    low_x, high_x = lax.ppermute(evens, "leaf", XP), lax.ppermute(evens, "leaf", XM)
    state = attend(0, work, qt, swapped(evens, odds), None)
    low, high, state = lax.optimization_barrier((low, high, state))
    pieces = swapped(low, high)
    low, high = along_z(low, high)
    state = attend(1, work, qt, pieces, state)
    low, high, low_x, high_x, state = lax.optimization_barrier((low, high, low_x, high_x, state))
    pieces = swapped(low, high, low_x)
    low, high = along_z(low, high)
    mid = low_x.shape[0] // 2
    far0 = lax.ppermute(low_x[:mid], "leaf", XP)
    far1 = lax.ppermute(high_x[mid:], "leaf", XM)
    state = attend(2, work, qt, pieces, state)
    low, high, high_x, state = lax.optimization_barrier((low, high, high_x, state))
    pieces = swapped(low, high, high_x)
    mid = low.shape[0] // 2
    low, high = along_z(low[:mid], high[mid:])
    state = attend(3, work, qt, pieces, state)
    low, high, far0, far1, state = lax.optimization_barrier((low, high, far0, far1, state))
    return attend(4, work, qt, swapped(low, high, far0, far1), state)[3]


def solution(mesh):
    in_specs = (
        P(("leaf", "ctx"), "head"),
        P(("leaf", "ctx"), "head"),
        P(None, "head"),
        P(None, "head"),
        P(),
        P(),
    )
    out_specs = P(("leaf", "ctx"), "head")
    return jax.shard_map(
        on_device, mesh=mesh, in_specs=in_specs, out_specs=out_specs, check_vma=False
    )
```

time: 208 us -> 218 us (1.048)
  the two profiles are of different devices: /device:TPU:37 before, /device:TPU:6 now
where the time goes in v1:
time: 218 us; the launch traced here: 216 us
  Pallas kernels  79.7 us (37%)
  starting transfers between devices  72.6 us (33%)
  waiting for transfers between devices  54.7 us (25%)
  local copies, waits for them, and re-layouts  7.89 us (4%)
    pallas_call x5, Pallas kernels, attend(): pl.pallas_call(functools.partial(attend_kernel, which, len(pieces)), in_s...  65.3 us
    ppermute x7, waiting for transfers between devices, on_device(): lax.ppermute(sends[s], 'ctx', turn(NZ, s))  31.6 us
    ppermute x7, starting transfers between devices, on_device(): lax.ppermute(sends[s], 'ctx', turn(NZ, s))  19 us
    ppermute x8, starting transfers between devices, along_z(): return (lax.ppermute(a, 'ctx', ZP), lax.ppermute(b, 'ctx', ZM))  12.2 us
    ppermute x3, starting transfers between devices, ring_z(): high = lax.ppermute(high, 'ctx', ZM)  10.6 us
    ppermute x1, starting transfers between devices, on_device(): far0 = lax.ppermute(low_x[:mid], 'leaf', XP)  10.6 us
    ppermute x8, waiting for transfers between devices, along_z(): return (lax.ppermute(a, 'ctx', ZP), lax.ppermute(b, 'ctx', ZM))  9.04 us
    pallas_call x1, Pallas kernels, walk(): pl.pallas_call(walk_kernel, in_specs=[smem()] * 4, out_specs=[smem()] * 3...  8.08 us
  transfers between devices with their start and end apart: 49, of which 16 were waited for; matrix products, arithmetic and copies ran while one was open for 1% of the time, Pallas kernels for 29%

profile of v1, /device:TPU:6, one launch (start us, length us, event | category | flops | bytes accessed | tf_op | source)
XLA Modules:
  0.0 216.3 jit_solution(3315920312571424879)
XLA Ops:
  0.0 1.6 collective-permute-start
  1.6 1.7 collective-permute-start.1
  3.3 1.2 copy-done.2
  4.5 0.7 copy-done.6
  5.2 2.3 %pack.1 = (bf16[2,32,2048]{2,1,0:T(8,128)(2,1)S(1)}, bf16[2,32,2048]{2,1,0:T(8,128)(2,1)S(1)}, bf16[2,32,2048]{2,1,0:T(8,128)(2,1)S(1)}, bf16[2,32,2048]{2,1,0:T...) custom-call(s32[3]{0:T(128)S(1)} %pad_add_fusion.where, ...), custom_call_target="tpu_custom_call" | custom-call | bytes 3145728 | tf_op jit(solution)/shard_map/pack/pallas_call | solution.py:80
  7.5 2.0 collective-permute-start.4
  9.5 3.3 %collective-permute-start.5 = (bf16[2,32,2048]{2,1,0:T(8,128)(2,1)S(1)}, bf16[2,32,2048]{2,1,0:T(8,128)(2,1)S(1)}, u32[]{:S(2)}, u32[]{:S(2)}) collective-permute-start(bf16[2,32,2048]{2,1,0:T(8,128)(2,1)S(1)} %get-tuple-element.79), channel_id=1, source_target_pairs={{0,8},{4,12},{8,16},{12,20},{16,24},{20,28},{24,0},{28,4},{1,9},{5... | collective-permute-start | bytes 786440 | tf_op jit(solution)/shard_map/ppermute | solution.py:390
  12.8 4.0 %collective-permute-start.6 = (bf16[2,32,2048]{2,1,0:T(8,128)(2,1)S(1)}, bf16[2,32,2048]{2,1,0:T(8,128)(2,1)S(1)}, u32[]{:S(2)}, u32[]{:S(2)}) collective-permute-start(bf16[2,32,2048]{2,1,0:T(8,128)(2,1)S(1)} %get-tuple-element.80), channel_id=1, source_target_pairs={{0,12},{4,16},{8,20},{12,24},{16,28},{20,0},{24,4},{28,8},{1,13},{... | collective-permute-start | bytes 786440 | tf_op jit(solution)/shard_map/ppermute | solution.py:390
  16.8 1.1 collective-permute-done.before
  18.0 0.7 slice.36
  18.7 1.6 collective-permute-start.2
  20.3 0.8 slice.37
  21.1 1.7 collective-permute-start.3
  22.7 6.7 %collective-permute-start.7 = (bf16[2,32,2048]{2,1,0:T(8,128)(2,1)}, bf16[2,32,2048]{2,1,0:T(8,128)(2,1)}, u32[]{:S(2)}, u32[]{:S(2)}) collective-permute-start(bf16[2,32,2048]{2,1,0:T(8,128)(2,1)} %get-tuple-element.82), channel_id=1, source_target_pairs={{0,20},{4,24},{8,28},{12,0},{16,4},{20,8},{24,12},{28,16},{1,21},{... | collective-permute-start | bytes 786440 | tf_op jit(solution)/shard_map/ppermute | solution.py:390
  29.5 7.3 %collective-permute-done.5.refs_2_ = bf16[2,32,2048]{2,1,0:T(8,128)(2,1)S(1)} collective-permute-done((bf16[2,32,2048]{2,1,0:T(8,128)(2,1)S(1)}, bf16[2,32,2048]{2,1,0:T(8,128)(2,1)S(1)}, u32[]{:S(2)}, u32[]{:S(2)}) %collective-permute-start.5) | collective-permute-done | bytes 262176 | tf_op jit(solution)/shard_map/ppermute | solution.py:390
  36.7 10.6 %collective-permute-done.6.refs_3_ = bf16[2,32,2048]{2,1,0:T(8,128)(2,1)S(1)} collective-permute-done((bf16[2,32,2048]{2,1,0:T(8,128)(2,1)S(1)}, bf16[2,32,2048]{2,1,0:T(8,128)(2,1)S(1)}, u32[]{:S(2)}, u32[]{:S(2)}) %collective-permute-start.6) | collective-permute-done | bytes 262176 | tf_op jit(solution)/shard_map/ppermute | solution.py:390
  47.3 0.7 copy-done.4
  48.0 0.6 fusion
  48.6 8.1 %walk.1 = (s32[1360]{0:T(1024)}, s32[340]{0:T(512)}, s32[5]{0:T(128)}) custom-call(s32[128]{0:T(128)} %parents.1, s32[8]{0:T(128)} %copy-done.7, s32[128]{0:T(128)} %get-tuple-element.153.which, s32[128]{0:T(128)} %get-tuple-element.154.place), custom_call_target="tpu_custom_call" | custom-call | bytes 16777216 | tf_op jit(solution)/shard_map/walk/pallas_call | solution.py:129
  56.7 2.9 %collective-permute-start.22 = (bf16[2,32,2048]{2,1,0:T(8,128)(2,1)}, bf16[2,32,2048]{2,1,0:T(8,128)(2,1)S(1)}, u32[]{:S(2)}, u32[]{:S(2)}) collective-permute-start(bf16[2,32,2048]{2,1,0:T(8,128)(2,1)} %copy-done.9), channel_id=1, source_target_pairs={{0,16},{4,20},{8,24},{12,28},{16,0},{20,4},{24,8},{28,12},{1,17},{... | collective-permute-start | bytes 786440 | tf_op jit(solution)/shard_map/ppermute | solution.py:390
  59.7 13.8 %collective-permute-done.9.refs_7_ = bf16[2,32,2048]{2,1,0:T(8,128)(2,1)} collective-permute-done((bf16[2,32,2048]{2,1,0:T(8,128)(2,1)}, bf16[2,32,2048]{2,1,0:T(8,128)(2,1)}, u32[]{:S(2)}, u32[]{:S(2)}) %collective-permute-start.9) | collective-permute-done | bytes 262176 | tf_op jit(solution)/shard_map/ppermute | solution.py:390
  73.4 1.7 copy-done
  75.2 1.7 copy-done.1
  76.9 2.1 project.1
  79.1 0.6 collective-permute-start.10
  79.7 1.5 collective-permute-start.11
  81.2 4.0 %collective-permute-start.15 = (bf16[256,256]{1,0:T(8,128)(2,1)S(1)}, bf16[256,256]{1,0:T(8,128)(2,1)S(1)}, u32[]{:S(2)}, u32[]{:S(2)}) collective-permute-start(bf16[256,256]{1,0:T(8,128)(2,1)S(1)} %get-tuple-element.149), channel_id=1, source_target_pairs={{0,28},{4,0},{8,4},{12,8},{16,12},{20,16},{24,20},{28,24},{1,29},{... | collective-permute-start | bytes 393224 | tf_op jit(solution)/shard_map/ppermute | solution.py:376
  85.2 2.0 unpack.1.qt
  87.3 1.8 collective-permute-start.12
  89.1 0.3 collective-permute-start.13
  89.4 3.3 %collective-permute-start.17 = (bf16[256,256]{1,0:T(8,128)(2,1)S(1)}, bf16[256,256]{1,0:T(8,128)(2,1)S(1)}, u32[]{:S(2)}, u32[]{:S(2)}) collective-permute-start(bf16[256,256]{1,0:T(8,128)(2,1)S(1)} %collective-permute-done.15), channel_id=1, source_target_pairs={{0,28},{4,0},{8,4},{12,8},{16,12},{20,16},{24,20},{28,24},{1,29},{... | collective-permute-start | bytes 393224 | tf_op jit(solution)/shard_map/ppermute | solution.py:376
  92.8 1.8 collective-permute-done.13
  94.5 1.0 collective-permute-done.16
  95.6 3.3 %collective-permute-start.19 = (bf16[256,256]{1,0:T(8,128)(2,1)S(1)}, bf16[256,256]{1,0:T(8,128)(2,1)S(1)}, u32[]{:S(2)}, u32[]{:S(2)}) collective-permute-start(bf16[256,256]{1,0:T(8,128)(2,1)S(1)} %collective-permute-done.17), channel_id=1, source_target_pairs={{0,28},{4,0},{8,4},{12,8},{16,12},{20,16},{24,20},{28,24},{1,29},{... | collective-permute-start | bytes 393224 | tf_op jit(solution)/shard_map/ppermute | solution.py:376
  99.0 3.4 %collective-permute-done.18 = bf16[256,256]{1,0:T(8,128)(2,1)S(1)} collective-permute-done((bf16[256,256]{1,0:T(8,128)(2,1)S(1)}, bf16[256,256]{1,0:T(8,128)(2,1)S(1)}, u32[]{:S(2)}, u32[]{:S(2)}) %collective-permute-start.18) | collective-permute-done | bytes 131104 | tf_op jit(solution)/shard_map/ppermute | solution.py:375
  102.4 3.4 %collective-permute-start.21 = (bf16[128,256]{1,0:T(8,128)(2,1)S(1)}, bf16[128,256]{1,0:T(8,128)(2,1)S(1)}, u32[]{:S(2)}, u32[]{:S(2)}) collective-permute-start(bf16[128,256]{1,0:T(8,128)(2,1)S(1)} %slice.51), channel_id=1, source_target_pairs={{0,28},{4,0},{8,4},{12,8},{16,12},{20,16},{24,20},{28,24},{1,29},{... | collective-permute-start | bytes 196616 | tf_op jit(solution)/shard_map/ppermute | solution.py:378
  105.8 2.0 collective-permute-done.20
  108.0 0.5 collective-permute-start.26
  108.5 3.3 %collective-permute-start.24 = (bf16[1024,256]{1,0:T(8,128)(2,1)S(1)}, bf16[1024,256]{1,0:T(8,128)(2,1)S(1)}, u32[]{:S(2)}, u32[]{:S(2)}) collective-permute-start(bf16[1024,256]{1,0:T(8,128)(2,1)S(1)} %constant_dynamic-update-slice_fusion), channel_id=1, source_target_pairs={{0,28},{4,0},{8,4},{12,8},{16,12},{20,16},{24,20},{28,24},{1,29},{... | collective-permute-start | bytes 1572872 | tf_op jit(solution)/shard_map/ppermute | solution.py:425
  111.8 2.9 %collective-permute-start.29 = (bf16[2048,256]{1,0:T(8,128)(2,1)S(1)}, bf16[2048,256]{1,0:T(8,128)(2,1)S(1)}, u32[]{:S(2)}, u32[]{:S(2)}) collective-permute-start(bf16[2048,256]{1,0:T(8,128)(2,1)S(1)} %constant_dynamic-update-slice_fusion.5), channel_id=1, source_target_pairs={{0,64},{32,96},{64,128},{96,160},{128,192},{160,224},{192,0},{224,... | collective-permute-start | bytes 3145736 | tf_op jit(solution)/shard_map/ppermute | solution.py:428
  114.8 14.0 %attend.5 = (f32[16,1,256]{2,1,0:T(1,128)S(1)}, f32[16,1,256]{2,1,0:T(1,128)S(1)}, f32[16,128,256]{2,1,0:T(8,128)S(1)}) custom-call(s32[1360]{0:T(1024)S(1)} %copy-done.10, s32[340]{0:T(512)S(1)} %copy-done.11, s32[5]{0:T(128)S(1)} %copy-done.12, s32[8]{0:T(128)S(1)} %copy-done.8, bf16[8,2,128,256]{3,2,1,0:T(8,128)(2,1)S(1)} %unpack.1.qt, ...), custom_call_target="tpu_custom_call" | custom-call | flops 2147483648 | bytes 6291456 | tf_op jit(solution)/shard_map/attend/pallas_call | solution.py:332
  128.8 0.1 collective-permute-start.32
  128.9 0.5 collective-permute-start.31
  129.4 1.4 collective-permute-done.32
  130.8 2.1 collective-permute-start.28
  132.8 7.3 %attend.6 = (f32[16,1,256]{2,1,0:T(1,128)S(1)}, f32[16,1,256]{2,1,0:T(1,128)S(1)}, f32[16,128,256]{2,1,0:T(8,128)S(1)}) custom-call(s32[1360]{0:T(1024)S(1)} %copy-done.10, s32[340]{0:T(512)S(1)} %copy-done.11, s32[5]{0:T(128)S(1)} %copy-done.12, s32[8]{0:T(128)S(1)} %copy-done.8, ...), custom_call_target="tpu_custom_call", output_to_operand_aliasing={{0}: (9, {}), {1}: (10, {}), {2}: (11, {})} | custom-call | flops 2147483648 | bytes 6291456 | tf_op jit(solution)/shard_map/attend/pallas_call | solution.py:332
  140.1 0.4 collective-permute-done.30
  140.5 4.0 %collective-permute-done.27 = bf16[1024,256]{1,0:T(8,128)(2,1)S(1)} collective-permute-done((bf16[1024,256]{1,0:T(8,128)(2,1)S(1)}, bf16[1024,256]{1,0:T(8,128)(2,1)S(1)}, u32[]{:S(2)}, u32[]{:S(2)}) %collective-permute-start.27) | collective-permute-done | bytes 524320 | tf_op jit(solution)/shard_map/ppermute | solution.py:425
  144.5 0.2 collective-permute-done.28
  144.7 0.5 collective-permute-start.35
  145.2 3.3 %collective-permute-start.34 = (bf16[1024,256]{1,0:T(8,128)(2,1)S(1)}, bf16[1024,256]{1,0:T(8,128)(2,1)S(1)}, u32[]{:S(2)}, u32[]{:S(2)}) collective-permute-start(bf16[1024,256]{1,0:T(8,128)(2,1)S(1)} %collective-permute-done.28), channel_id=1, source_target_pairs={{0,28},{4,0},{8,4},{12,8},{16,12},{20,16},{24,20},{28,24},{1,29},{... | collective-permute-start | bytes 1572872 | tf_op jit(solution)/shard_map/ppermute | solution.py:425
  148.5 0.4 collective-permute-done.36
  148.9 7.4 %attend.7 = (f32[16,1,256]{2,1,0:T(1,128)S(1)}, f32[16,1,256]{2,1,0:T(1,128)S(1)}, f32[16,128,256]{2,1,0:T(8,128)S(1)}) custom-call(s32[1360]{0:T(1024)S(1)} %copy-done.10, s32[340]{0:T(512)S(1)} %copy-done.11, s32[5]{0:T(128)S(1)} %copy-done.12, s32[8]{0:T(128)S(1)} %copy-done.8, ...), custom_call_target="tpu_custom_call", output_to_operand_aliasing={{0}: (11, {}), {1}: (12, {}), {2}: (13, {})} | custom-call | flops 2147483648 | bytes 6291456 | tf_op jit(solution)/shard_map/attend/pallas_call | solution.py:332
  156.3 4.8 %collective-permute-done.33 = bf16[1024,256]{1,0:T(8,128)(2,1)S(1)} collective-permute-done((bf16[1024,256]{1,0:T(8,128)(2,1)S(1)}, bf16[1024,256]{1,0:T(8,128)(2,1)S(1)}, u32[]{:S(2)}, u32[]{:S(2)}) %collective-permute-start.33) | collective-permute-done | bytes 524320 | tf_op jit(solution)/shard_map/ppermute | solution.py:425
  161.1 0.5 collective-permute-start.42
  161.7 10.6 %collective-permute-start.40 = (bf16[1024,256]{1,0:T(8,128)(2,1)S(1)}, bf16[1024,256]{1,0:T(8,128)(2,1)S(1)}, u32[]{:S(2)}, u32[]{:S(2)}) collective-permute-start(bf16[1024,256]{1,0:T(8,128)(2,1)S(1)} %slice.46), channel_id=1, source_target_pairs={{0,64},{32,96},{64,128},{96,160},{128,192},{160,224},{192,0},{224,... | collective-permute-start | bytes 1572872 | tf_op jit(solution)/shard_map/ppermute | solution.py:438
  172.4 3.5 %collective-permute-start.39 = (bf16[512,256]{1,0:T(8,128)(2,1)S(1)}, bf16[512,256]{1,0:T(8,128)(2,1)S(1)}, u32[]{:S(2)}, u32[]{:S(2)}) collective-permute-start(bf16[512,256]{1,0:T(8,128)(2,1)S(1)} %slice.45), channel_id=1, source_target_pairs={{0,28},{4,0},{8,4},{12,8},{16,12},{20,16},{24,20},{28,24},{1,29},{... | collective-permute-start | bytes 786440 | tf_op jit(solution)/shard_map/ppermute | solution.py:425
  175.9 19.9 %attend.8 = (f32[16,1,256]{2,1,0:T(1,128)S(1)}, f32[16,1,256]{2,1,0:T(1,128)S(1)}, f32[16,128,256]{2,1,0:T(8,128)S(1)}) custom-call(s32[1360]{0:T(1024)S(1)} %copy-done.10, s32[340]{0:T(512)S(1)} %copy-done.11, s32[5]{0:T(128)S(1)} %copy-done.12, s32[8]{0:T(128)S(1)} %copy-done.8, ...), custom_call_target="tpu_custom_call", output_to_operand_aliasing={{0}: (11, {}), {1}: (12, {}), {2}: (13, {})} | custom-call | flops 2147483648 | bytes 6291456 | tf_op jit(solution)/shard_map/attend/pallas_call | solution.py:332
  196.0 0.5 collective-permute-start.48
  196.5 0.1 collective-permute-start.45
  196.6 0.4 collective-permute-start.46
  197.0 2.0 collective-permute-done.45
  199.0 0.4 collective-permute-done.46
  199.4 16.7 %attend.9 = (f32[16,1,256]{2,1,0:T(1,128)S(1)}, f32[16,1,256]{2,1,0:T(1,128)S(1)}, f32[16,128,256]{2,1,0:T(8,128)S(1)}, bf16[256,2048]{1,0:T(8,128)(2,1)}) custom-call(s32[1360]{0:T(1024)S(1)} %copy-done.10, s32[340]{0:T(512)S(1)} %copy-done.11, s32[5]{0:T(128)S(1)} %copy-done.12, ...), custom_call_target="tpu_custom_call", output_to_operand_aliasing={{0}: (13, {}), {1}: (14, {}), {2}: (15, {})} | custom-call | flops 2147483648 | bytes 6291456 | tf_op jit(solution)/shard_map/attend/pallas_call | solution.py:332
  (94 shorter events, 0.8 us)
Async XLA Ops:
  0.0 18.0 %collective-permute-start = (bf16[256,1280]{1,0:T(8,128)(2,1)}, bf16[256,1280]{1,0:T(8,128)(2,1)S(1)}, u32[]{:S(2)}, u32[]{:S(2)}) collective-permute-start(bf16[256,1280]{1,0:T(8,128)(2,1)} %own), channel_id=1, source_target_pairs={{0,1},{1,2},{2,3},{3,0},{4,5},{5,6},{6,7},{7,4},{8,9},{9,10},{10,1... | collective-permute-start | bytes 1966088 | tf_op jit(solution)/shard_map/ppermute | solution.py:362
  1.6 16.4 %collective-permute-start.1 = (bf16[256,1280]{1,0:T(8,128)(2,1)}, bf16[256,1280]{1,0:T(8,128)(2,1)S(1)}, u32[]{:S(2)}, u32[]{:S(2)}) collective-permute-start(bf16[256,1280]{1,0:T(8,128)(2,1)} %own), channel_id=1, source_target_pairs={{0,3},{1,0},{2,1},{3,2},{4,7},{5,4},{6,5},{7,6},{8,11},{9,8},{10,9... | collective-permute-start | bytes 1966088 | tf_op jit(solution)/shard_map/ppermute | solution.py:363
  3.3 1.2 copy-start.2
  4.5 0.7 copy-start.6
  5.2 68.2 %copy-start.3 = (bf16[256,1280]{1,0:T(8,128)(2,1)S(1)}, bf16[256,1280]{1,0:T(8,128)(2,1)}, u32[]{:S(2)}) copy-start(bf16[256,1280]{1,0:T(8,128)(2,1)} %own) | copy-start | bytes 1966084
  7.5 39.8 %copy-start.7 = (s32[8]{0:T(128)}, s32[8]{0:T(128)S(1)}, u32[]{:S(2)}) copy-start(s32[8]{0:T(128)S(1)} %get-tuple-element.87.info) | copy-start | bytes 100
  7.5 39.8 %copy-start.9 = (bf16[2,32,2048]{2,1,0:T(8,128)(2,1)}, bf16[2,32,2048]{2,1,0:T(8,128)(2,1)S(1)}, u32[]{:S(2)}) copy-start(bf16[2,32,2048]{2,1,0:T(8,128)(2,1)S(1)} %get-tuple-element.81) | copy-start | bytes 786436
  7.5 15.2 %collective-permute-start.4 = (bf16[2,32,2048]{2,1,0:T(8,128)(2,1)S(1)}, bf16[2,32,2048]{2,1,0:T(8,128)(2,1)S(1)}, u32[]{:S(2)}, u32[]{:S(2)}) collective-permute-start(bf16[2,32,2048]{2,1,0:T(8,128)(2,1)S(1)} %get-tuple-element.78), channel_id=1, source_target_pairs={{0,4},{4,8},{8,12},{12,16},{16,20},{20,24},{24,28},{28,0},{1,5},{5... | collective-permute-start | bytes 786440 | tf_op jit(solution)/shard_map/ppermute | solution.py:390
  9.5 27.2 %collective-permute-start.5 = (bf16[2,32,2048]{2,1,0:T(8,128)(2,1)S(1)}, bf16[2,32,2048]{2,1,0:T(8,128)(2,1)S(1)}, u32[]{:S(2)}, u32[]{:S(2)}) collective-permute-start(bf16[2,32,2048]{2,1,0:T(8,128)(2,1)S(1)} %get-tuple-element.79), channel_id=1, source_target_pairs={{0,8},{4,12},{8,16},{12,20},{16,24},{20,28},{24,0},{28,4},{1,9},{5... | collective-permute-start | bytes 786440 | tf_op jit(solution)/shard_map/ppermute | solution.py:390
  12.8 34.5 %collective-permute-start.6 = (bf16[2,32,2048]{2,1,0:T(8,128)(2,1)S(1)}, bf16[2,32,2048]{2,1,0:T(8,128)(2,1)S(1)}, u32[]{:S(2)}, u32[]{:S(2)}) collective-permute-start(bf16[2,32,2048]{2,1,0:T(8,128)(2,1)S(1)} %get-tuple-element.80), channel_id=1, source_target_pairs={{0,12},{4,16},{8,20},{12,24},{16,28},{20,0},{24,4},{28,8},{1,13},{... | collective-permute-start | bytes 786440 | tf_op jit(solution)/shard_map/ppermute | solution.py:390
  18.7 54.7 %collective-permute-start.2 = (bf16[128,1280]{1,0:T(8,128)(2,1)}, bf16[128,1280]{1,0:T(8,128)(2,1)S(1)}, u32[]{:S(2)}, u32[]{:S(2)}) collective-permute-start(bf16[128,1280]{1,0:T(8,128)(2,1)} %slice.36), channel_id=1, source_target_pairs={{0,1},{1,2},{2,3},{3,0},{4,5},{5,6},{6,7},{7,4},{8,9},{9,10},{10,1... | collective-permute-start | bytes 983048 | tf_op jit(solution)/shard_map/ppermute | solution.py:365
  21.1 52.4 %collective-permute-start.3 = (bf16[128,1280]{1,0:T(8,128)(2,1)}, bf16[128,1280]{1,0:T(8,128)(2,1)S(1)}, u32[]{:S(2)}, u32[]{:S(2)}) collective-permute-start(bf16[128,1280]{1,0:T(8,128)(2,1)} %slice.37), channel_id=1, source_target_pairs={{0,3},{1,0},{2,1},{3,2},{4,7},{5,4},{6,5},{7,6},{8,11},{9,8},{10,9... | collective-permute-start | bytes 983048 | tf_op jit(solution)/shard_map/ppermute | solution.py:366
  22.7 34.0 %collective-permute-start.7 = (bf16[2,32,2048]{2,1,0:T(8,128)(2,1)}, bf16[2,32,2048]{2,1,0:T(8,128)(2,1)}, u32[]{:S(2)}, u32[]{:S(2)}) collective-permute-start(bf16[2,32,2048]{2,1,0:T(8,128)(2,1)} %get-tuple-element.82), channel_id=1, source_target_pairs={{0,20},{4,24},{8,28},{12,0},{16,4},{20,8},{24,12},{28,16},{1,21},{... | collective-permute-start | bytes 786440 | tf_op jit(solution)/shard_map/ppermute | solution.py:390
  36.7 22.9 %collective-permute-start.8 = (bf16[2,32,2048]{2,1,0:T(8,128)(2,1)}, bf16[2,32,2048]{2,1,0:T(8,128)(2,1)}, u32[]{:S(2)}, u32[]{:S(2)}) collective-permute-start(bf16[2,32,2048]{2,1,0:T(8,128)(2,1)} %get-tuple-element.83), channel_id=1, source_target_pairs={{0,24},{4,28},{8,0},{12,4},{16,8},{20,12},{24,16},{28,20},{1,25},{... | collective-permute-start | bytes 786440 | tf_op jit(solution)/shard_map/ppermute | solution.py:390
  47.3 0.7 copy-start.4
  48.0 25.4 %collective-permute-start.9 = (bf16[2,32,2048]{2,1,0:T(8,128)(2,1)}, bf16[2,32,2048]{2,1,0:T(8,128)(2,1)}, u32[]{:S(2)}, u32[]{:S(2)}) collective-permute-start(bf16[2,32,2048]{2,1,0:T(8,128)(2,1)} %get-tuple-element.84), channel_id=1, source_target_pairs={{0,28},{4,0},{8,4},{12,8},{16,12},{20,16},{24,20},{28,24},{1,29},{... | collective-permute-start | bytes 786440 | tf_op jit(solution)/shard_map/ppermute | solution.py:390
  56.7 28.5 %collective-permute-start.22 = (bf16[2,32,2048]{2,1,0:T(8,128)(2,1)}, bf16[2,32,2048]{2,1,0:T(8,128)(2,1)S(1)}, u32[]{:S(2)}, u32[]{:S(2)}) collective-permute-start(bf16[2,32,2048]{2,1,0:T(8,128)(2,1)} %copy-done.9), channel_id=1, source_target_pairs={{0,16},{4,20},{8,24},{12,28},{16,0},{20,4},{24,8},{28,12},{1,17},{... | collective-permute-start | bytes 786440 | tf_op jit(solution)/shard_map/ppermute | solution.py:390
  73.4 1.7 copy-start
  75.2 1.7 copy-start.1
  76.9 8.3 %copy-start.5 = (bf16[2,32,2048]{2,1,0:T(8,128)(2,1)S(1)}, bf16[2,32,2048]{2,1,0:T(8,128)(2,1)}, u32[]{:S(2)}) copy-start(bf16[2,32,2048]{2,1,0:T(8,128)(2,1)} %copy-done.4) | copy-start | bytes 786436
  79.1 8.1 %collective-permute-start.10 = (bf16[256,256]{1,0:T(8,128)(2,1)S(1)}, bf16[256,256]{1,0:T(8,128)(2,1)S(1)}, u32[]{:S(2)}, u32[]{:S(2)}) collective-permute-start(bf16[256,256]{1,0:T(8,128)(2,1)S(1)} %get-tuple-element.152), channel_id=1, source_target_pairs={{0,64},{32,96},{64,128},{96,160},{128,192},{160,224},{192,0},{224,... | collective-permute-start | bytes 393224 | tf_op jit(solution)/shard_map/ppermute | solution.py:362
  79.7 7.6 %collective-permute-start.11 = (bf16[256,256]{1,0:T(8,128)(2,1)S(1)}, bf16[256,256]{1,0:T(8,128)(2,1)S(1)}, u32[]{:S(2)}, u32[]{:S(2)}) collective-permute-start(bf16[256,256]{1,0:T(8,128)(2,1)S(1)} %get-tuple-element.152), channel_id=1, source_target_pairs={{0,192},{32,224},{64,0},{96,32},{128,64},{160,96},{192,128},{224,1... | collective-permute-start | bytes 393224 | tf_op jit(solution)/shard_map/ppermute | solution.py:363
  81.2 8.2 %collective-permute-start.14 = (bf16[256,256]{1,0:T(8,128)(2,1)S(1)}, bf16[256,256]{1,0:T(8,128)(2,1)S(1)}, u32[]{:S(2)}, u32[]{:S(2)}) collective-permute-start(bf16[256,256]{1,0:T(8,128)(2,1)S(1)} %get-tuple-element.149), channel_id=1, source_target_pairs={{0,4},{4,8},{8,12},{12,16},{16,20},{20,24},{24,28},{28,0},{1,5},{5... | collective-permute-start | bytes 393224 | tf_op jit(solution)/shard_map/ppermute | solution.py:375
  81.2 8.2 %collective-permute-start.15 = (bf16[256,256]{1,0:T(8,128)(2,1)S(1)}, bf16[256,256]{1,0:T(8,128)(2,1)S(1)}, u32[]{:S(2)}, u32[]{:S(2)}) collective-permute-start(bf16[256,256]{1,0:T(8,128)(2,1)S(1)} %get-tuple-element.149), channel_id=1, source_target_pairs={{0,28},{4,0},{8,4},{12,8},{16,12},{20,16},{24,20},{28,24},{1,29},{... | collective-permute-start | bytes 393224 | tf_op jit(solution)/shard_map/ppermute | solution.py:376
  87.2 27.5 %copy-start.8 = (s32[8]{0:T(128)S(1)}, s32[8]{0:T(128)}, u32[]{:S(2)}) copy-start(s32[8]{0:T(128)} %copy-done.7) | copy-start | bytes 100
  87.2 27.5 %copy-start.10 = (s32[1360]{0:T(1024)S(1)}, s32[1360]{0:T(1024)}, u32[]{:S(2)}) copy-start(s32[1360]{0:T(1024)} %get-tuple-element.91.lists) | copy-start | bytes 16324
  87.2 27.5 %copy-start.11 = (s32[340]{0:T(512)S(1)}, s32[340]{0:T(512)}, u32[]{:S(2)}) copy-start(s32[340]{0:T(512)} %get-tuple-element.92.tiles) | copy-start | bytes 4084
  87.2 27.5 %copy-start.12 = (s32[5]{0:T(128)S(1)}, s32[5]{0:T(128)}, u32[]{:S(2)}) copy-start(s32[5]{0:T(128)} %get-tuple-element.93.counts) | copy-start | bytes 64
  87.3 5.5 %collective-permute-start.12 = (bf16[128,256]{1,0:T(8,128)(2,1)S(1)}, bf16[128,256]{1,0:T(8,128)(2,1)S(1)}, u32[]{:S(2)}, u32[]{:S(2)}) collective-permute-start(bf16[128,256]{1,0:T(8,128)(2,1)S(1)} %slice.39), channel_id=1, source_target_pairs={{0,64},{32,96},{64,128},{96,160},{128,192},{160,224},{192,0},{224,... | collective-permute-start | bytes 196616 | tf_op jit(solution)/shard_map/ppermute | solution.py:365
  89.1 5.5 %collective-permute-start.13 = (bf16[128,256]{1,0:T(8,128)(2,1)S(1)}, bf16[128,256]{1,0:T(8,128)(2,1)S(1)}, u32[]{:S(2)}, u32[]{:S(2)}) collective-permute-start(bf16[128,256]{1,0:T(8,128)(2,1)S(1)} %slice.40), channel_id=1, source_target_pairs={{0,192},{32,224},{64,0},{96,32},{128,64},{160,96},{192,128},{224,1... | collective-permute-start | bytes 196616 | tf_op jit(solution)/shard_map/ppermute | solution.py:366
  89.4 6.2 %collective-permute-start.16 = (bf16[256,256]{1,0:T(8,128)(2,1)S(1)}, bf16[256,256]{1,0:T(8,128)(2,1)S(1)}, u32[]{:S(2)}, u32[]{:S(2)}) collective-permute-start(bf16[256,256]{1,0:T(8,128)(2,1)S(1)} %collective-permute-done.14), channel_id=1, source_target_pairs={{0,4},{4,8},{8,12},{12,16},{16,20},{20,24},{24,28},{28,0},{1,5},{5... | collective-permute-start | bytes 393224 | tf_op jit(solution)/shard_map/ppermute | solution.py:375
  89.4 6.2 %collective-permute-start.17 = (bf16[256,256]{1,0:T(8,128)(2,1)S(1)}, bf16[256,256]{1,0:T(8,128)(2,1)S(1)}, u32[]{:S(2)}, u32[]{:S(2)}) collective-permute-start(bf16[256,256]{1,0:T(8,128)(2,1)S(1)} %collective-permute-done.15), channel_id=1, source_target_pairs={{0,28},{4,0},{8,4},{12,8},{16,12},{20,16},{24,20},{28,24},{1,29},{... | collective-permute-start | bytes 393224 | tf_op jit(solution)/shard_map/ppermute | solution.py:376
  95.6 6.8 %collective-permute-start.18 = (bf16[256,256]{1,0:T(8,128)(2,1)S(1)}, bf16[256,256]{1,0:T(8,128)(2,1)S(1)}, u32[]{:S(2)}, u32[]{:S(2)}) collective-permute-start(bf16[256,256]{1,0:T(8,128)(2,1)S(1)} %collective-permute-done.16), channel_id=1, source_target_pairs={{0,4},{4,8},{8,12},{12,16},{16,20},{20,24},{24,28},{28,0},{1,5},{5... | collective-permute-start | bytes 393224 | tf_op jit(solution)/shard_map/ppermute | solution.py:375
  95.6 6.8 %collective-permute-start.19 = (bf16[256,256]{1,0:T(8,128)(2,1)S(1)}, bf16[256,256]{1,0:T(8,128)(2,1)S(1)}, u32[]{:S(2)}, u32[]{:S(2)}) collective-permute-start(bf16[256,256]{1,0:T(8,128)(2,1)S(1)} %collective-permute-done.17), channel_id=1, source_target_pairs={{0,28},{4,0},{8,4},{12,8},{16,12},{20,16},{24,20},{28,24},{1,29},{... | collective-permute-start | bytes 393224 | tf_op jit(solution)/shard_map/ppermute | solution.py:376
  102.4 5.5 %collective-permute-start.20 = (bf16[128,256]{1,0:T(8,128)(2,1)S(1)}, bf16[128,256]{1,0:T(8,128)(2,1)S(1)}, u32[]{:S(2)}, u32[]{:S(2)}) collective-permute-start(bf16[128,256]{1,0:T(8,128)(2,1)S(1)} %slice.50), channel_id=1, source_target_pairs={{0,4},{4,8},{8,12},{12,16},{16,20},{20,24},{24,28},{28,0},{1,5},{5... | collective-permute-start | bytes 196616 | tf_op jit(solution)/shard_map/ppermute | solution.py:378
  102.4 5.5 %collective-permute-start.21 = (bf16[128,256]{1,0:T(8,128)(2,1)S(1)}, bf16[128,256]{1,0:T(8,128)(2,1)S(1)}, u32[]{:S(2)}, u32[]{:S(2)}) collective-permute-start(bf16[128,256]{1,0:T(8,128)(2,1)S(1)} %slice.51), channel_id=1, source_target_pairs={{0,28},{4,0},{8,4},{12,8},{16,12},{20,16},{24,20},{28,24},{1,29},{... | collective-permute-start | bytes 196616 | tf_op jit(solution)/shard_map/ppermute | solution.py:378
  107.9 6.8 %collective-permute-start.25 = (bf16[2048,256]{1,0:T(8,128)(2,1)S(1)}, bf16[2048,256]{1,0:T(8,128)(2,1)S(1)}, u32[]{:S(2)}, u32[]{:S(2)}) collective-permute-start(bf16[2048,256]{1,0:T(8,128)(2,1)S(1)} %constant_dynamic-update-slice_fusion.5), channel_id=1, source_target_pairs={{0,32},{32,0},{64,96},{96,64},{128,160},{160,128},{192,224},{224,1... | collective-permute-start | bytes 3145736 | tf_op jit(solution)/shard_map/ppermute | solution.py:382
  108.0 6.7 %collective-permute-start.26 = (bf16[1024,256]{1,0:T(8,128)(2,1)S(1)}, bf16[1024,256]{1,0:T(8,128)(2,1)S(1)}, u32[]{:S(2)}, u32[]{:S(2)}) collective-permute-start(bf16[1024,256]{1,0:T(8,128)(2,1)S(1)} %constant_dynamic-update-slice_fusion), channel_id=1, source_target_pairs={{0,32},{32,0},{64,96},{96,64},{128,160},{160,128},{192,224},{224,1... | collective-permute-start | bytes 1572872 | tf_op jit(solution)/shard_map/ppermute | solution.py:382
  108.5 20.2 %collective-permute-start.23 = (bf16[1024,256]{1,0:T(8,128)(2,1)S(1)}, bf16[1024,256]{1,0:T(8,128)(2,1)S(1)}, u32[]{:S(2)}, u32[]{:S(2)}) collective-permute-start(bf16[1024,256]{1,0:T(8,128)(2,1)S(1)} %constant_dynamic-update-slice_fusion), channel_id=1, source_target_pairs={{0,4},{4,8},{8,12},{12,16},{16,20},{20,24},{24,28},{28,0},{1,5},{5... | collective-permute-start | bytes 1572872 | tf_op jit(solution)/shard_map/ppermute | solution.py:425
  108.5 20.2 %collective-permute-start.24 = (bf16[1024,256]{1,0:T(8,128)(2,1)S(1)}, bf16[1024,256]{1,0:T(8,128)(2,1)S(1)}, u32[]{:S(2)}, u32[]{:S(2)}) collective-permute-start(bf16[1024,256]{1,0:T(8,128)(2,1)S(1)} %constant_dynamic-update-slice_fusion), channel_id=1, source_target_pairs={{0,28},{4,0},{8,4},{12,8},{16,12},{20,16},{24,20},{28,24},{1,29},{... | collective-permute-start | bytes 1572872 | tf_op jit(solution)/shard_map/ppermute | solution.py:425
  111.8 28.3 %collective-permute-start.29 = (bf16[2048,256]{1,0:T(8,128)(2,1)S(1)}, bf16[2048,256]{1,0:T(8,128)(2,1)S(1)}, u32[]{:S(2)}, u32[]{:S(2)}) collective-permute-start(bf16[2048,256]{1,0:T(8,128)(2,1)S(1)} %constant_dynamic-update-slice_fusion.5), channel_id=1, source_target_pairs={{0,64},{32,96},{64,128},{96,160},{128,192},{160,224},{192,0},{224,... | collective-permute-start | bytes 3145736 | tf_op jit(solution)/shard_map/ppermute | solution.py:428
  114.7 25.8 %collective-permute-start.30 = (bf16[2048,256]{1,0:T(8,128)(2,1)S(1)}, bf16[2048,256]{1,0:T(8,128)(2,1)S(1)}, u32[]{:S(2)}, u32[]{:S(2)}) collective-permute-start(bf16[2048,256]{1,0:T(8,128)(2,1)S(1)} %constant_dynamic-update-slice_fusion.5), channel_id=1, source_target_pairs={{0,192},{32,224},{64,0},{96,32},{128,64},{160,96},{192,128},{224,1... | collective-permute-start | bytes 3145736 | tf_op jit(solution)/shard_map/ppermute | solution.py:428
  128.8 2.0 collective-permute-start.32
  128.9 4.0 %collective-permute-start.31 = (bf16[1024,256]{1,0:T(8,128)(2,1)S(1)}, bf16[1024,256]{1,0:T(8,128)(2,1)S(1)}, u32[]{:S(2)}, u32[]{:S(2)}) collective-permute-start(bf16[1024,256]{1,0:T(8,128)(2,1)S(1)} %collective-permute-done.23), channel_id=1, source_target_pairs={{0,32},{32,0},{64,96},{96,64},{128,160},{160,128},{192,224},{224,1... | collective-permute-start | bytes 1572872 | tf_op jit(solution)/shard_map/ppermute | solution.py:382
  129.4 15.1 %collective-permute-start.27 = (bf16[1024,256]{1,0:T(8,128)(2,1)S(1)}, bf16[1024,256]{1,0:T(8,128)(2,1)S(1)}, u32[]{:S(2)}, u32[]{:S(2)}) collective-permute-start(bf16[1024,256]{1,0:T(8,128)(2,1)S(1)} %collective-permute-done.23), channel_id=1, source_target_pairs={{0,4},{4,8},{8,12},{12,16},{16,20},{20,24},{24,28},{28,0},{1,5},{5... | collective-permute-start | bytes 1572872 | tf_op jit(solution)/shard_map/ppermute | solution.py:425
  130.8 14.0 %collective-permute-start.28 = (bf16[1024,256]{1,0:T(8,128)(2,1)S(1)}, bf16[1024,256]{1,0:T(8,128)(2,1)S(1)}, u32[]{:S(2)}, u32[]{:S(2)}) collective-permute-start(bf16[1024,256]{1,0:T(8,128)(2,1)S(1)} %collective-permute-done.24), channel_id=1, source_target_pairs={{0,28},{4,0},{8,4},{12,8},{16,12},{20,16},{24,20},{28,24},{1,29},{... | collective-permute-start | bytes 1572872 | tf_op jit(solution)/shard_map/ppermute | solution.py:425
  144.7 4.2 %collective-permute-start.37 = (bf16[2048,256]{1,0:T(8,128)(2,1)S(1)}, bf16[2048,256]{1,0:T(8,128)(2,1)S(1)}, u32[]{:S(2)}, u32[]{:S(2)}) collective-permute-start(bf16[2048,256]{1,0:T(8,128)(2,1)S(1)} %collective-permute-done.29), channel_id=1, source_target_pairs={{0,32},{32,0},{64,96},{96,64},{128,160},{160,128},{192,224},{224,1... | collective-permute-start | bytes 3145736 | tf_op jit(solution)/shard_map/ppermute | solution.py:382
  144.7 3.8 %collective-permute-start.35 = (bf16[1024,256]{1,0:T(8,128)(2,1)S(1)}, bf16[1024,256]{1,0:T(8,128)(2,1)S(1)}, u32[]{:S(2)}, u32[]{:S(2)}) collective-permute-start(bf16[1024,256]{1,0:T(8,128)(2,1)S(1)} %collective-permute-done.27), channel_id=1, source_target_pairs={{0,32},{32,0},{64,96},{96,64},{128,160},{160,128},{192,224},{224,1... | collective-permute-start | bytes 1572872 | tf_op jit(solution)/shard_map/ppermute | solution.py:382
  145.2 3.6 %collective-permute-start.36 = (bf16[1024,256]{1,0:T(8,128)(2,1)S(1)}, bf16[1024,256]{1,0:T(8,128)(2,1)S(1)}, u32[]{:S(2)}, u32[]{:S(2)}) collective-permute-start(bf16[1024,256]{1,0:T(8,128)(2,1)S(1)} %collective-permute-done.28), channel_id=1, source_target_pairs={{0,32},{32,0},{64,96},{96,64},{128,160},{160,128},{192,224},{224,1... | collective-permute-start | bytes 1572872 | tf_op jit(solution)/shard_map/ppermute | solution.py:382
  145.2 15.9 %collective-permute-start.33 = (bf16[1024,256]{1,0:T(8,128)(2,1)S(1)}, bf16[1024,256]{1,0:T(8,128)(2,1)S(1)}, u32[]{:S(2)}, u32[]{:S(2)}) collective-permute-start(bf16[1024,256]{1,0:T(8,128)(2,1)S(1)} %collective-permute-done.27), channel_id=1, source_target_pairs={{0,4},{4,8},{8,12},{12,16},{16,20},{20,24},{24,28},{28,0},{1,5},{5... | collective-permute-start | bytes 1572872 | tf_op jit(solution)/shard_map/ppermute | solution.py:425
  145.2 15.9 %collective-permute-start.34 = (bf16[1024,256]{1,0:T(8,128)(2,1)S(1)}, bf16[1024,256]{1,0:T(8,128)(2,1)S(1)}, u32[]{:S(2)}, u32[]{:S(2)}) collective-permute-start(bf16[1024,256]{1,0:T(8,128)(2,1)S(1)} %collective-permute-done.28), channel_id=1, source_target_pairs={{0,28},{4,0},{8,4},{12,8},{16,12},{20,16},{24,20},{28,24},{1,29},{... | collective-permute-start | bytes 1572872 | tf_op jit(solution)/shard_map/ppermute | solution.py:425
  161.1 14.8 %collective-permute-start.44 = (bf16[2048,256]{1,0:T(8,128)(2,1)S(1)}, bf16[2048,256]{1,0:T(8,128)(2,1)S(1)}, u32[]{:S(2)}, u32[]{:S(2)}) collective-permute-start(bf16[2048,256]{1,0:T(8,128)(2,1)S(1)} %collective-permute-done.30), channel_id=1, source_target_pairs={{0,32},{32,0},{64,96},{96,64},{128,160},{160,128},{192,224},{224,1... | collective-permute-start | bytes 3145736 | tf_op jit(solution)/shard_map/ppermute | solution.py:382
  161.1 11.2 %collective-permute-start.42 = (bf16[1024,256]{1,0:T(8,128)(2,1)S(1)}, bf16[1024,256]{1,0:T(8,128)(2,1)S(1)}, u32[]{:S(2)}, u32[]{:S(2)}) collective-permute-start(bf16[1024,256]{1,0:T(8,128)(2,1)S(1)} %collective-permute-done.33), channel_id=1, source_target_pairs={{0,32},{32,0},{64,96},{96,64},{128,160},{160,128},{192,224},{224,1... | collective-permute-start | bytes 1572872 | tf_op jit(solution)/shard_map/ppermute | solution.py:382
  161.6 10.8 %collective-permute-start.43 = (bf16[1024,256]{1,0:T(8,128)(2,1)S(1)}, bf16[1024,256]{1,0:T(8,128)(2,1)S(1)}, u32[]{:S(2)}, u32[]{:S(2)}) collective-permute-start(bf16[1024,256]{1,0:T(8,128)(2,1)S(1)} %collective-permute-done.34), channel_id=1, source_target_pairs={{0,32},{32,0},{64,96},{96,64},{128,160},{160,128},{192,224},{224,1... | collective-permute-start | bytes 1572872 | tf_op jit(solution)/shard_map/ppermute | solution.py:382
  161.7 34.1 %collective-permute-start.40 = (bf16[1024,256]{1,0:T(8,128)(2,1)S(1)}, bf16[1024,256]{1,0:T(8,128)(2,1)S(1)}, u32[]{:S(2)}, u32[]{:S(2)}) collective-permute-start(bf16[1024,256]{1,0:T(8,128)(2,1)S(1)} %slice.46), channel_id=1, source_target_pairs={{0,64},{32,96},{64,128},{96,160},{128,192},{160,224},{192,0},{224,... | collective-permute-start | bytes 1572872 | tf_op jit(solution)/shard_map/ppermute | solution.py:438
  172.3 23.6 %collective-permute-start.41 = (bf16[1024,256]{1,0:T(8,128)(2,1)S(1)}, bf16[1024,256]{1,0:T(8,128)(2,1)S(1)}, u32[]{:S(2)}, u32[]{:S(2)}) collective-permute-start(bf16[1024,256]{1,0:T(8,128)(2,1)S(1)} %slice.47), channel_id=1, source_target_pairs={{0,192},{32,224},{64,0},{96,32},{128,64},{160,96},{192,128},{224,1... | collective-permute-start | bytes 1572872 | tf_op jit(solution)/shard_map/ppermute | solution.py:439
  172.3 23.5 %collective-permute-start.38 = (bf16[512,256]{1,0:T(8,128)(2,1)S(1)}, bf16[512,256]{1,0:T(8,128)(2,1)S(1)}, u32[]{:S(2)}, u32[]{:S(2)}) collective-permute-start(bf16[512,256]{1,0:T(8,128)(2,1)S(1)} %slice.44), channel_id=1, source_target_pairs={{0,4},{4,8},{8,12},{12,16},{16,20},{20,24},{24,28},{28,0},{1,5},{5... | collective-permute-start | bytes 786440 | tf_op jit(solution)/shard_map/ppermute | solution.py:425
  172.4 23.5 %collective-permute-start.39 = (bf16[512,256]{1,0:T(8,128)(2,1)S(1)}, bf16[512,256]{1,0:T(8,128)(2,1)S(1)}, u32[]{:S(2)}, u32[]{:S(2)}) collective-permute-start(bf16[512,256]{1,0:T(8,128)(2,1)S(1)} %slice.45), channel_id=1, source_target_pairs={{0,28},{4,0},{8,4},{12,8},{16,12},{20,16},{24,20},{28,24},{1,29},{... | collective-permute-start | bytes 786440 | tf_op jit(solution)/shard_map/ppermute | solution.py:425
  195.9 3.5 %collective-permute-start.47 = (bf16[1024,256]{1,0:T(8,128)(2,1)S(1)}, bf16[1024,256]{1,0:T(8,128)(2,1)S(1)}, u32[]{:S(2)}, u32[]{:S(2)}) collective-permute-start(bf16[1024,256]{1,0:T(8,128)(2,1)S(1)} %collective-permute-done.40), channel_id=1, source_target_pairs={{0,32},{32,0},{64,96},{96,64},{128,160},{160,128},{192,224},{224,1... | collective-permute-start | bytes 1572872 | tf_op jit(solution)/shard_map/ppermute | solution.py:382
  196.0 3.4 %collective-permute-start.48 = (bf16[1024,256]{1,0:T(8,128)(2,1)S(1)}, bf16[1024,256]{1,0:T(8,128)(2,1)S(1)}, u32[]{:S(2)}, u32[]{:S(2)}) collective-permute-start(bf16[1024,256]{1,0:T(8,128)(2,1)S(1)} %collective-permute-done.41), channel_id=1, source_target_pairs={{0,32},{32,0},{64,96},{96,64},{128,160},{160,128},{192,224},{224,1... | collective-permute-start | bytes 1572872 | tf_op jit(solution)/shard_map/ppermute | solution.py:382
  196.5 2.5 %collective-permute-start.45 = (bf16[512,256]{1,0:T(8,128)(2,1)S(1)}, bf16[512,256]{1,0:T(8,128)(2,1)S(1)}, u32[]{:S(2)}, u32[]{:S(2)}) collective-permute-start(bf16[512,256]{1,0:T(8,128)(2,1)S(1)} %collective-permute-done.38), channel_id=1, source_target_pairs={{0,32},{32,0},{64,96},{96,64},{128,160},{160,128},{192,224},{224,1... | collective-permute-start | bytes 786440 | tf_op jit(solution)/shard_map/ppermute | solution.py:382
  196.6 2.8 %collective-permute-start.46 = (bf16[512,256]{1,0:T(8,128)(2,1)S(1)}, bf16[512,256]{1,0:T(8,128)(2,1)S(1)}, u32[]{:S(2)}, u32[]{:S(2)}) collective-permute-start(bf16[512,256]{1,0:T(8,128)(2,1)S(1)} %collective-permute-done.39), channel_id=1, source_target_pairs={{0,32},{32,0},{64,96},{96,64},{128,160},{160,128},{192,224},{224,1... | collective-permute-start | bytes 786440 | tf_op jit(solution)/shard_map/ppermute | solution.py:382
